TPU v7x, 512 devices: a whole 4x4x16 slice. The times are simulated.
512 devices in a mesh: fib: 128 (over y, z, core), run: 4 (over x).
Axes of the slice: x: 4, y: 4, z: 16, core: 2. Of those that a mesh axis runs over, the one named last changes fastest.
Arguments:
- slab: bfloat16 [4, 512, 16384], P('run', 'fib'), may hold values from -6 to 6
- chord_weight: float32 [512], P('fib'), may hold values from 0.3 to 3
- span_weight: float32 [256], replicated, may hold values from 0.1 to 1
- start: float32 [512, 64], replicated, may hold values from -6 to 6
Outputs:
- core_unfolding: bfloat16 [4, 4096, 256], P('run', 'fib')
All inputs are finite; a program needn't handle non-finite values.
Results may differ from a plain program's by a relative error of at most 0.0048.
The roundings to bfloat16 on the way count: a program that leaves them out, or rounds other values in their place, can miss the bound.
Values may be sent and summed in bfloat16 or wider, within the bound.
No kernel may reach another device: no remote copies, remote signals or barrier semaphores. Data moves between devices by JAX's collectives and lax.ppermute only.
A program may use at most 64 MiB of HBM per device.

v0:
```python
import jax
import jax.numpy as jnp
from jax import lax
from jax.sharding import PartitionSpec as P

K = 64
ITERS = 3


def orthonormal(matrix):
    small = jnp.dot(
        matrix.T, matrix, precision=lax.Precision.HIGHEST, preferred_element_type=jnp.float32
    )
    lower_tri = jnp.linalg.cholesky(small)
    return lax.linalg.triangular_solve(
        lower_tri, matrix, left_side=False, lower=True, transpose_a=True
    )


def per_device(slab, chord_weight, span_weight, start):
    run_count = slab.shape[0]
    stations = jnp.repeat(span_weight, K)
    weighted = (slab.astype(jnp.float32) * chord_weight[:, None] * stations[None, :]).astype(
        jnp.bfloat16
    )
    fibres = lax.all_to_all(weighted, "fib", split_axis=2, concat_axis=1, tiled=True)
    factor = start
    local_gram = jnp.einsum("rcj,rdj->cd", fibres, fibres, preferred_element_type=jnp.float32)
    gram = lax.psum(local_gram, ("fib", "run"))
    for iteration in range(ITERS):
        product = jnp.dot(
            gram, factor, precision=lax.Precision.HIGHEST, preferred_element_type=jnp.float32
        )
        factor = orthonormal(product)
    narrow = factor.astype(jnp.bfloat16)
    rank_count = narrow.shape[1]
    span_local = fibres.shape[2] // K
    core_block = jnp.einsum(
        "ca,rcj->raj", narrow, fibres, preferred_element_type=jnp.float32
    ).astype(jnp.bfloat16)
    arranged = core_block.reshape(run_count, rank_count, span_local, K).transpose(0, 1, 3, 2)
    arranged = arranged.reshape(run_count, rank_count * K, span_local)
    return lax.all_to_all(arranged, "fib", split_axis=1, concat_axis=2, tiled=True)


def solution(mesh):
    return jax.shard_map(
        per_device,
        mesh=mesh,
        in_specs=(P("run", "fib", None), P("fib"), P(), P()),
        out_specs=P("run", "fib", None),
        check_vma=False,
    )
```

profile of v0, /device:TPU:1, one launch (start us, length us, event | category | flops | bytes accessed | tf_op | source)
XLA Modules:
  0.0 823.5 jit_solution(8880804122961737390)
XLA Ops:
  6.5 0.8 broadcast_in_dim.4
  7.4 1.0 multiply_convert_fusion
  8.5 12.9 %copy.40 = bf16[1,4,16384]{1,0,2:T(2,128)(2,1)} copy(bf16[1,4,16384]{2,1,0:T(4,128)(2,1)S(1)} %multiply_convert_fusion) | data formatting | bytes 262144 | tf_op jit(solution)/shard_map/convert_element_type | solution.py:23
  21.4 0.5 broadcast.40
  21.9 90.8 %reduce.4 = bf16[16384,4]{1,0:T(8,128)(2,1)} reduce(bf16[16384,1,4]{2,1,0:T(2,128)(2,1)} %bitcast.81, bf16[]{:T(256)} %broadcast.40), dimensions={1}, to_apply=%bitcast.57.reduce_sub_computation | reduce | bytes 262146
  112.7 8.7 %reshape.46 = bf16[128,2,256]{2,1,0:T(2,128)(2,1)S(1)} reshape(bf16[16384,4]{1,0:T(8,128)(2,1)} %reduce.4) | data formatting | bytes 262144
  121.3 37.7 %all_to_all.33 = bf16[128,2,256]{2,1,0:T(2,128)(2,1)S(1)} all-to-all(bf16[128,2,256]{2,1,0:T(2,128)(2,1)S(1)} %reshape.46), channel_id=1, replica_groups=mesh['fib'=128,'run'=4] {'fib'}, dimensions={0} | all-to-all | bytes 262144 | tf_op jit(solution)/shard_map/all_to_all | solution.py:26
  159.0 17.1 %reshape.47 = bf16[16384,1,4]{2,1,0:T(2,128)(2,1)} reshape(bf16[128,2,256]{2,1,0:T(2,128)(2,1)S(1)} %all_to_all.33) | data formatting | bytes 262144
  176.1 15.4 %copy.41 = bf16[1,4,16384]{2,1,0:T(4,128)(2,1)S(1)} copy(bf16[1,4,16384]{1,0,2:T(2,128)(2,1)} %bitcast.82) | data formatting | bytes 262144 | tf_op jit(solution)/shard_map/all_to_all | solution.py:26
  191.6 1.3 fusion.15
  193.0 458.1 %all-reduce.2.cloned.1.call-done = f32[512,512]{1,0:T(8,128)} async-done(((f32[512,512]{1,0:T(8,128)}), f32[512,512]{1,0:T(8,128)}) %all-reduce.2.cloned.1.call-update) | async-done | bytes 1048592 | tf_op jit(solution)/shard_map/psum | solution.py:29
  651.1 2.4 fusion.16
  653.9 5.8 cholesky.59
  659.8 0.6 compare_reduce_fusion.2
  660.5 0.7 fusion.2
  661.1 4.9 custom-call.7
  666.0 0.3 convolution_bitcast_fusion.2
  666.4 2.4 fusion.18
  669.1 5.8 cholesky.70
  675.0 0.6 compare_reduce_fusion.1
  675.6 0.7 fusion.3
  676.3 4.9 custom-call.8
  681.5 1.1 fusion.20
  683.0 5.8 cholesky.81
  688.9 0.6 compare_reduce_fusion
  689.5 0.7 fusion.4
  690.2 4.9 custom-call.9
  695.1 0.3 fusion
  695.8 2.7 copy.47
  698.5 112.7 %all_to_all.34 = bf16[1,4096,2]{2,0,1:T(2,128)(2,1)} all-to-all(bf16[1,4096,2]{2,0,1:T(2,128)(2,1)S(1)} %copy.47), channel_id=1, replica_groups=mesh['fib'=128,'run'=4] {'fib'}, dimensions={1} | all-to-all | bytes 32768 | tf_op jit(solution)/shard_map/all_to_all | solution.py:43
  811.2 4.5 copy.48
  815.9 0.7 copy.50
  (28 shorter events, 2.2 us)
Async XLA Ops:
  6.5 644.6 %copy-start = (f32[512,64]{0,1:T(8,128)S(1)}, f32[512,64]{0,1:T(8,128)}, u32[]{:S(2)}) copy-start(f32[512,64]{0,1:T(8,128)} %param.10) | copy-start | bytes 393220
  6.5 644.6 %all-reduce.2.cloned.1.call-start = ((), (), s32[]{:S(2)}) async-start(), calls=%async_computation.2 | async-start | bytes 2097152 | tf_op jit(solution)/shard_map/psum | solution.py:29
  651.1 30.4 %copy-start.1 = (f32[512,512]{1,0:T(8,128)S(1)}, f32[512,512]{1,0:T(8,128)}, u32[]{:S(2)}) copy-start(f32[512,512]{1,0:T(8,128)} %all-reduce.2.cloned.1.call-done) | copy-start | bytes 3145732
Sparse Core Ops, SparseCore 0:
  193.1 457.9 all-reduce.1
where the time goes:
time: 824 us; the launch traced here: 823 us
  waiting for transfers between devices  458 us (56%)
  blocking collectives  150 us (18%)
  other arithmetic  128 us (16%)
  local copies, waits for them, and re-layouts  64.1 us (8%)
  between operations  13.6 us (2%)
  matrix products  9.22 us (1%)
    psum x1, waiting for transfers between devices, per_device(): gram = lax.psum(local_gram, ('fib', 'run'))  458 us
    all_to_all x1, blocking collectives, per_device(): lax.all_to_all(arranged, 'fib', split_axis=1, concat_axis=2, tiled=True)  113 us
    unnamed x1, other arithmetic  90.8 us
    all_to_all x1, blocking collectives, per_device(): lax.all_to_all(weighted, 'fib', split_axis=2, concat_axis=1, tiled=True)  37.7 us
    unnamed x8, local copies, waits for them, and re-layouts  26.3 us
    another operation x9, other arithmetic, orthonormal(): lower_tri = jnp.linalg.cholesky(small)  19.6 us
    another operation x6, other arithmetic, orthonormal(): lax.linalg.triangular_solve(lower_tri, matrix, left_side=False, lower=Tru...  16.6 us
  transfers between devices with their start and end apart: 1, of which 1 were waited for; matrix products, arithmetic and copies ran while one was open for 0% of the time, Pallas kernels for 0%

commit v1 on v0

v1 whole, which is shorter than its diff:
```python
import jax
import jax.numpy as jnp
from jax import lax
from jax.experimental import pallas as pl
from jax.experimental.pallas import tpu as pltpu
from jax.sharding import Mesh, PartitionSpec as P

K = 64
ITERS = 3
LANES = 128
HIGHEST = lax.Precision.HIGHEST
VMEM = pl.BlockSpec(memory_space=pltpu.VMEM)
FIB = ("y", "z", "core")
PLANE = ("y", "core", "run")
PAIRS = [(i, j) for i in range(4) for j in range(i, 4)]


def call(kernel, shape, dtype, scratch=()):
    return pl.pallas_call(
        kernel,
        out_shape=jax.ShapeDtypeStruct(shape, dtype),
        out_specs=VMEM,
        scratch_shapes=scratch,
        compiler_params=pltpu.CompilerParams(vmem_limit_bytes=32 * 1024 * 1024),
    )


def nn(a, b, precision=None):
    return lax.dot_general(
        a, b, (((1,), (0,)), ((), ())), precision=precision, preferred_element_type=jnp.float32
    )


def nt(a, b, precision=None):
    return lax.dot_general(
        a, b, (((1,), (1,)), ((), ())), precision=precision, preferred_element_type=jnp.float32
    )


def tn(a, b, precision=None):
    return lax.dot_general(
        a, b, (((0,), (0,)), ((), ())), precision=precision, preferred_element_type=jnp.float32
    )


def weigh_kernel(slab_ref, chord_ref, span_ref, out_ref):
    lane = lax.broadcasted_iota(jnp.int32, (1, LANES), 1)
    chord = chord_ref[...]
    for tile in range(out_ref.shape[0]):
        stations = jnp.where(
            lane < K, span_ref[tile : tile + 1, 0:1], span_ref[tile : tile + 1, 1:2]
        )
        block = slab_ref[0, :, tile * LANES : (tile + 1) * LANES].astype(jnp.float32)
        out_ref[tile] = (block * chord * stations).astype(jnp.bfloat16)


def gram_kernel(fibres_ref, out_ref):
    for at, (i, j) in enumerate(PAIRS):
        out_ref[at * 128 : (at + 1) * 128, :] = nt(
            fibres_ref[i * 128 : (i + 1) * 128, :], fibres_ref[j * 128 : (j + 1) * 128, :]
        )


def inverse_cholesky(small):
    n = small.shape[0]
    eye = lax.broadcasted_iota(jnp.int32, (n, n), 0) == lax.broadcasted_iota(jnp.int32, (n, n), 1)
    both = jnp.concatenate([small, eye.astype(jnp.float32)], axis=1)
    blocks = [both[8 * b : 8 * b + 8] for b in range(n // 8)]
    sub = lax.broadcasted_iota(jnp.int32, (8, 1), 0)
    lane = lax.broadcasted_iota(jnp.int32, (8, 2 * n), 1)
    for j in range(n):
        own, i = divmod(j, 8)
        row = blocks[own][i : i + 1]
        row = row * (1.0 / row[:, j : j + 1])
        for b in range(own, n // 8):
            column = blocks[b][:, j : j + 1]
            if b == own:
                if i == 7:
                    continue
                column = jnp.where(sub > i, column, 0.0)
            blocks[b] = blocks[b] - column * row
    rows = []
    for b in range(n // 8):
        pivot = jnp.sum(jnp.where(lane == sub + 8 * b, blocks[b], 0.0), axis=1, keepdims=True)
        rows.append(blocks[b][:, n:] * lax.rsqrt(pivot))
    return jnp.concatenate(rows, axis=0)


def factor_kernel(packed_ref, start_ref, fibres_ref, out_ref, gram_ref):
    for at, (i, j) in enumerate(PAIRS):
        block = packed_ref[at * 128 : (at + 1) * 128, :]
        gram_ref[i * 128 : (i + 1) * 128, j * 128 : (j + 1) * 128] = block
        if i != j:
            gram_ref[j * 128 : (j + 1) * 128, i * 128 : (i + 1) * 128] = block.T
    factor = start_ref[...]
    for _ in range(ITERS):
        product = nn(factor, gram_ref[...], HIGHEST)
        small = nt(product, product, HIGHEST)
        factor = nn(inverse_cholesky(small), product, HIGHEST)
    core = nn(factor.astype(jnp.bfloat16), fibres_ref[...])
    rank = core.shape[0]
    for half in range(2):
        low = core[:, half * 32 : half * 32 + 32]
        high = core[:, K + half * 32 : K + half * 32 + 32]
        out_ref[half * rank : (half + 1) * rank, :] = jnp.concatenate([low, high], axis=1).astype(
            jnp.bfloat16
        )


def unfold_kernel(parts_ref, out_ref):
    senders = parts_ref.shape[0]
    row = lax.broadcasted_iota(jnp.int32, (senders, 2 * senders), 0)
    station = lax.broadcasted_iota(jnp.int32, (senders, 2 * senders), 1)
    half = senders // 2
    pair = jnp.where(row < half, 2 * row, 2 * (row - half) + 1)
    out = None
    for parity in range(2):
        place = (station == 2 * pair + parity).astype(jnp.bfloat16)
        term = tn(parts_ref[:, parity * 32 : parity * 32 + 32], place)
        out = term if out is None else out + term
    out_ref[0] = out.astype(jnp.bfloat16)


def swap(array, axes):
    return lax.all_to_all(array, axes, 0, 0, tiled=True)


def sum_everywhere(packed):
    rows = packed.shape[0] // 32
    part = swap(packed.reshape(32, rows, LANES), PLANE).sum(0)
    deep = -(-rows // 16)
    part = jnp.pad(part, ((0, 16 * deep - rows), (0, 0))).reshape(16, deep, LANES)
    part = swap(part, "z").sum(0)
    part = swap(jnp.broadcast_to(part[None], (16, deep, LANES)), "z")
    part = part.reshape(16 * deep, LANES)[:rows]
    return swap(jnp.broadcast_to(part[None], (32, rows, LANES)), PLANE).reshape(packed.shape)


def per_device(slab, chord_weight, span_weight, start):
    rows, columns = slab.shape[1:]
    tiles = columns // LANES
    send = call(weigh_kernel, (tiles, rows, LANES), jnp.bfloat16)(
        slab, chord_weight[:, None], span_weight.reshape(tiles, 2)
    )
    fibres = swap(send, FIB).reshape(tiles * rows, LANES)
    packed = call(gram_kernel, (len(PAIRS) * 128, 128), jnp.float32)(fibres)
    packed = sum_everywhere(packed)
    chords, rank = start.shape
    parts = call(
        factor_kernel,
        (2 * rank, K),
        jnp.bfloat16,
        [pltpu.VMEM((chords, chords), jnp.float32)],
    )(packed, start.T, fibres)
    parts = swap(parts.reshape(2 * rank, 1, K), ("core", "y", "z")).reshape(2 * rank, K)
    return call(unfold_kernel, (1, 32, 2 * tiles), jnp.bfloat16)(parts)


def solution(mesh):
    fine = Mesh(mesh.devices.reshape(4, 16, 2, 4), FIB + ("run",))
    return jax.shard_map(
        per_device,
        mesh=fine,
        in_specs=(P("run", FIB, None), P(FIB), P(), P()),
        out_specs=P("run", FIB, None),
        check_vma=False,
    )
```

time: 824 us -> 149 us (0.18)
  waiting for transfers between devices: 458 us -> 0 us
  other arithmetic: 128 us -> 0.08 us
  local copies, waits for them, and re-layouts: 64.1 us -> 2.53 us
  blocking collectives: 150 us -> 125 us
  Pallas kernels: 0 us -> 21.4 us
  between operations: 13.6 us -> 0.07 us
  matrix products: 9.22 us -> 0 us
    psum x1 -> x0, waiting for transfers between devices: 458 us -> none  [per_device(): gram = lax.psum(local_gram, ('fib', 'run'))]
    unnamed x1 -> x0, other arithmetic: 90.8 us -> none
    another operation x15 -> x0, other arithmetic: 36.2 us -> none  [the longest x9 19.6 us: orthonormal(): lower_tri = jnp.linalg.cholesky(small)]
    all_to_all x2 -> x6, blocking collectives: 150 us -> 125 us  [swap(): return lax.all_to_all(array, axes, 0, 0, tiled=True)]
    unnamed x8, local copies, waits for them, and re-layouts: 26.3 us -> 2.15 us
    pallas_call x0 -> x4, Pallas kernels: none -> 21.4 us  [the longest x1 19.7 us: per_device(): call(factor_kernel, (2 * rank, K), jnp.bfloat16, [pltpu.VMEM((chords, cho...]
    all_to_all x6 -> x0, local copies, waits for them, and re-layouts: 20.9 us -> none  [the longest x2 15.5 us: per_device(): lax.all_to_all(weighted, 'fib', split_axis=2, concat_axis=1, tiled=True)]
    convert_element_type x1 -> x0, local copies, waits for them, and re-layouts: 12.9 us -> none  [per_device(): (slab.astype(jnp.float32) * chord_weight[:, None] * stations[None, :]).as...]
  transfers between devices with their start and end apart: 1 -> 0, of which waited for: 1 -> 0; matrix products, arithmetic and copies ran while one was open for 0% -> 0% of each run, Pallas kernels for 0% -> 0%
where the time goes in v1:
time: 149 us
  blocking collectives  125 us (84%)
  Pallas kernels  21.4 us (14%)
  local copies, waits for them, and re-layouts  2.53 us (2%)
    all_to_all x6, blocking collectives, swap(): return lax.all_to_all(array, axes, 0, 0, tiled=True)  125 us
    pallas_call x1, Pallas kernels, per_device(): call(factor_kernel, (2 * rank, K), jnp.bfloat16, [pltpu.VMEM((chords, cho...  19.7 us

profile of v1, /device:TPU:1, one launch (start us, length us, event | category | flops | bytes accessed | tf_op | source)
XLA Modules:
  0.0 149.0 jit_solution(10149432807121855860)
XLA Ops:
  0.0 0.0 copy-start.3
  0.0 0.7 copy-done.3
  0.7 0.0 copy-start.2
  0.7 0.1 copy.9.chord_ref
  0.8 0.6 copy-done.2
  1.3 0.1 reshape.26.span_ref
  1.5 0.0 copy-start
  1.5 0.9 copy-done
  2.4 0.5 shard_map.46
  2.9 37.7 %all_to_all.30 = bf16[128,4,128]{2,1,0:T(4,128)(2,1)S(1)} all-to-all(bf16[128,4,128]{2,1,0:T(4,128)(2,1)S(1)} %shard_map.46), channel_id=1, replica_groups=mesh['y'=4,'z'=16,'core'=2,'run'=4] {'y','z','core'}, dimensions={0} | all-to-all | bytes 262144 | tf_op jit(solution)/shard_map/all_to_all | solution.py:125
  40.6 0.3 shard_map.47
  40.9 19.7 %all_to_all.31 = f32[32,40,128]{2,1,0:T(8,128)S(1)} all-to-all(f32[32,40,128]{2,1,0:T(8,128)S(1)} %bitcast.11), channel_id=1, replica_groups=mesh['y'=4,'z'=16,'core'=2,'run'=4] {'y','core','run'}, dimensions={0} | all-to-all | bytes 1310720 | tf_op jit(solution)/shard_map/all_to_all | solution.py:125
  60.6 0.1 reduce_sum.18
  60.6 14.0 %all_to_all.32 = f32[16,3,128]{2,1,0:T(4,128)S(1)} all-to-all(f32[16,3,128]{2,1,0:T(4,128)S(1)} %reshape.29), channel_id=1, replica_groups=mesh['y'=4,'z'=16,'core'=2,'run'=4] {'z'}, dimensions={0} | all-to-all | bytes 49152 | tf_op jit(solution)/shard_map/all_to_all | solution.py:125
  74.6 14.0 %all_to_all.33 = f32[16,3,128]{2,1,0:T(4,128)S(1)} all-to-all(f32[16,3,128]{2,1,0:T(4,128)S(1)} %broadcast_in_dim.7), channel_id=1, replica_groups=mesh['y'=4,'z'=16,'core'=2,'run'=4] {'z'}, dimensions={0} | all-to-all | bytes 49152 | tf_op jit(solution)/shard_map/all_to_all | solution.py:125
  88.7 0.0 copy-start.1
  88.7 19.4 %all_to_all.34 = f32[32,40,128]{2,1,0:T(8,128)S(1)} all-to-all(f32[32,40,128]{2,1,0:T(8,128)S(1)} %broadcast_in_dim.8), channel_id=1, replica_groups=mesh['y'=4,'z'=16,'core'=2,'run'=4] {'y','core','run'}, dimensions={0} | all-to-all | bytes 1310720 | tf_op jit(solution)/shard_map/all_to_all | solution.py:125
  108.1 0.0 copy-done.1
  108.1 19.7 %shard_map.48 = bf16[128,64]{1,0:T(8,128)(2,1)S(1)} custom-call(f32[1280,128]{1,0:T(8,128)S(1)} %bitcast.10, f32[64,512]{1,0:T(8,128)S(1)} %bitcast.15, bf16[512,128]{1,0:T(8,128)(2,1)S(1)} %bitcast.13), custom_call_target="tpu_custom_call" | custom-call | tf_op jit(solution)/shard_map/pallas_call | solution.py:149
  127.8 0.1 copy.10
  127.8 20.3 %all_to_all.35 = bf16[128,1,64]{2,1,0:T(2,128)(2,1)S(1)} all-to-all(bf16[128,1,64]{2,1,0:T(2,128)(2,1)S(1)} %copy.10), channel_id=1, replica_groups=mesh['y'=4,'z'=16,'core'=2,'run'=4] {'core','y','z'}, dimensions={0} | all-to-all | bytes 32768 | tf_op jit(solution)/shard_map/all_to_all | solution.py:125
  148.1 0.8 shard_map.49
  (8 shorter events, 0.1 us)
Async XLA Ops:
  0.0 0.7 copy-start.3
  0.7 0.7 copy-start.2
  1.5 0.9 copy-start
  88.7 19.4 %copy-start.1 = (f32[512,64]{0,1:T(8,128)S(1)}, f32[512,64]{0,1:T(8,128)}, u32[]{:S(2)}) copy-start(f32[512,64]{0,1:T(8,128)} %param.7) | copy-start | bytes 393220

commit v2 on v1

v2 whole, which is shorter than its diff:
```python
import jax
import jax.numpy as jnp
from jax import lax
from jax.experimental import pallas as pl
from jax.experimental.pallas import tpu as pltpu
from jax.sharding import Mesh, PartitionSpec as P

K = 64
ITERS = 3
LANES = 128
HIGHEST = lax.Precision.HIGHEST
VMEM = pl.BlockSpec(memory_space=pltpu.VMEM)
SMEM = pl.BlockSpec(memory_space=pltpu.SMEM)
FIB = ("y", "z", "core")
PLANE = ("y", "core", "run")
PAIRS = [(i, j) for i in range(4) for j in range(i, 4)]


def call(kernel, shape, dtype, specs, scratch=()):
    return pl.pallas_call(
        kernel,
        out_shape=jax.ShapeDtypeStruct(shape, dtype),
        in_specs=specs,
        out_specs=VMEM,
        scratch_shapes=scratch,
        compiler_params=pltpu.CompilerParams(vmem_limit_bytes=32 * 1024 * 1024),
    )


def nn(a, b, precision=None):
    return lax.dot_general(
        a, b, (((1,), (0,)), ((), ())), precision=precision, preferred_element_type=jnp.float32
    )


def nt(a, b, precision=None):
    return lax.dot_general(
        a, b, (((1,), (1,)), ((), ())), precision=precision, preferred_element_type=jnp.float32
    )


def tn(a, b, precision=None):
    return lax.dot_general(
        a, b, (((0,), (0,)), ((), ())), precision=precision, preferred_element_type=jnp.float32
    )


def weigh_kernel(slab_ref, chord_ref, span_ref, out_ref):
    lane = lax.broadcasted_iota(jnp.int32, (1, LANES), 1)
    row = lax.broadcasted_iota(jnp.int32, (out_ref.shape[1], LANES), 0)
    chord = jnp.zeros(row.shape, jnp.float32)
    for i in range(out_ref.shape[1]):
        chord = jnp.where(row == i, chord_ref[i], chord)

    def weigh(tile):
        stations = jnp.where(lane < K, span_ref[2 * tile], span_ref[2 * tile + 1])
        block = slab_ref[0, :, tile * LANES : (tile + 1) * LANES].astype(jnp.float32)
        return block * chord * stations

    low_half = lane % K < K // 2
    for chip in range(out_ref.shape[0] // 2):
        first, second = weigh(2 * chip), weigh(2 * chip + 1)
        low = jnp.where(low_half, first, pltpu.roll(second, K // 2, 1))
        high = jnp.where(low_half, pltpu.roll(first, LANES - K // 2, 1), second)
        out_ref[2 * chip] = low.astype(jnp.bfloat16)
        out_ref[2 * chip + 1] = high.astype(jnp.bfloat16)


def gram_kernel(fibres_ref, out_ref):
    for at, (i, j) in enumerate(PAIRS):
        out_ref[at * 128 : (at + 1) * 128, :] = nt(
            fibres_ref[i * 128 : (i + 1) * 128, :], fibres_ref[j * 128 : (j + 1) * 128, :]
        )


def inverse_cholesky(small):
    n = small.shape[0]
    wide = (8, 2 * n)
    eye = lax.broadcasted_iota(jnp.int32, (n, n), 0) == lax.broadcasted_iota(jnp.int32, (n, n), 1)
    both = jnp.concatenate([small, eye.astype(jnp.float32)], axis=1)
    blocks = [both[8 * b : 8 * b + 8] for b in range(n // 8)]
    sub = lax.broadcasted_iota(jnp.int32, wide, 0)
    rows = []
    for own in range(n // 8):
        panel = [
            {
                b: jnp.broadcast_to(blocks[b][:, 8 * own + k : 8 * own + k + 1], wide)
                for b in range(own, n // 8)
            }
            for k in range(8)
        ]
        pivots = None
        for k in range(8):
            pivot = jnp.broadcast_to(panel[k][own][k : k + 1], wide)
            pivots = pivot if pivots is None else jnp.where(sub >= k, pivot, pivots)
            inverse = 1.0 / pivot
            row = jnp.broadcast_to(blocks[own][k : k + 1], wide) * inverse
            column = dict(panel[k])
            column[own] = jnp.where(sub > k, column[own], 0.0)
            for later in range(k + 1, 8):
                scale = jnp.broadcast_to(panel[later][own][k : k + 1], wide) * inverse
                for b in range(own, n // 8):
                    panel[later][b] = panel[later][b] - column[b] * scale
            for b in range(own, n // 8):
                blocks[b] = blocks[b] - column[b] * row
        rows.append(blocks[own][:, n:] * lax.rsqrt(pivots)[:, n:])
    return jnp.concatenate(rows, axis=0)


def factor_kernel(packed_ref, start_ref, fibres_ref, out_ref, gram_ref):
    for at, (i, j) in enumerate(PAIRS):
        block = packed_ref[at * 128 : (at + 1) * 128, :]
        gram_ref[i * 128 : (i + 1) * 128, j * 128 : (j + 1) * 128] = block
        if i != j:
            gram_ref[j * 128 : (j + 1) * 128, i * 128 : (i + 1) * 128] = block.T
    factor = start_ref[...]
    for _ in range(ITERS):
        product = nn(factor, gram_ref[...], HIGHEST)
        small = nt(product, product, HIGHEST)
        factor = nn(inverse_cholesky(small), product, HIGHEST)
    core = nn(factor.astype(jnp.bfloat16), fibres_ref[...])
    out_ref[...] = core.astype(jnp.bfloat16).astype(jnp.float32)


def unfold_kernel(parts_ref, out_ref):
    chips = parts_ref.shape[0]
    chip = lax.broadcasted_iota(jnp.int32, (chips, 4 * chips), 0)
    station = lax.broadcasted_iota(jnp.int32, (chips, 4 * chips), 1)
    parts = parts_ref[...].astype(jnp.bfloat16)
    out = None
    for at in range(4):
        place = (station == 4 * chip + at).astype(jnp.bfloat16)
        lane = K * (at % 2) + K // 2 * (at // 2)
        term = tn(parts[:, lane : lane + K // 2], place)
        out = term if out is None else out + term
    out_ref[0] = out.astype(jnp.bfloat16)


def swap(array, axes):
    return lax.all_to_all(array, axes, 0, 0, tiled=True)


def sum_everywhere(packed):
    rows = packed.shape[0] // 32
    part = swap(packed.reshape(32, rows, LANES), PLANE).sum(0)
    part = swap(jnp.broadcast_to(part[None], (16, rows, LANES)), "z").sum(0)
    return swap(jnp.broadcast_to(part[None], (32, rows, LANES)), PLANE).reshape(packed.shape)


def per_device(slab, chord_weight, span_weight, start):
    rows, columns = slab.shape[1:]
    tiles = columns // LANES
    send = call(weigh_kernel, (tiles, rows, LANES), jnp.bfloat16, [VMEM, SMEM, SMEM])(
        slab, chord_weight, span_weight
    )
    fibres = swap(send, FIB).reshape(tiles * rows, LANES)
    packed = call(gram_kernel, (len(PAIRS) * 128, 128), jnp.float32, [VMEM])(fibres)
    packed = sum_everywhere(packed)
    chords, rank = start.shape
    parts = call(
        factor_kernel,
        (rank, LANES),
        jnp.float32,
        [VMEM] * 3,
        [pltpu.VMEM((chords, chords), jnp.float32)],
    )(packed, start.T, fibres)
    parts = swap(parts.reshape(rank, 1, LANES), ("y", "z")).reshape(rank, LANES)
    return call(unfold_kernel, (1, K // 2, 4 * rank), jnp.bfloat16, [VMEM])(parts)


def solution(mesh):
    fine = Mesh(mesh.devices.reshape(4, 16, 2, 4), FIB + ("run",))
    return jax.shard_map(
        per_device,
        mesh=fine,
        in_specs=(P("run", FIB, None), P(FIB), P(), P()),
        out_specs=P("run", FIB, None),
        check_vma=False,
    )
```

time: 149 us -> 133 us (0.89)
  Pallas kernels: 21.4 us -> 11 us
  blocking collectives: 125 us -> 119 us
    pallas_call x4, Pallas kernels: 21.4 us -> 11 us  [the longest x1 9.06 us: per_device(): call(factor_kernel, (rank, LANES), jnp.float32, [VMEM] * 3, [pltpu.VMEM((...]
    all_to_all x6 -> x5, blocking collectives: 125 us -> 119 us  [swap(): return lax.all_to_all(array, axes, 0, 0, tiled=True)]
where the time goes in v2:
time: 133 us; the launch traced here: 132 us
  blocking collectives  119 us (89%)
  Pallas kernels  11 us (8%)
  local copies, waits for them, and re-layouts  2.31 us (2%)
    all_to_all x5, blocking collectives, swap(): return lax.all_to_all(array, axes, 0, 0, tiled=True)  119 us
    pallas_call x1, Pallas kernels, per_device(): call(factor_kernel, (rank, LANES), jnp.float32, [VMEM] * 3, [pltpu.VMEM((...  9.06 us

profile of v2, /device:TPU:1, one launch (start us, length us, event | category | flops | bytes accessed | tf_op | source)
XLA Modules:
  0.0 132.3 jit_solution(3924565899521020016)
XLA Ops:
  0.0 0.0 copy-start
  0.0 0.9 copy-done
  0.9 0.0 copy-start.2
  0.9 0.7 copy-done.2
  1.6 0.0 copy-start.3
  1.6 0.7 copy-done.3
  2.2 0.7 shard_map.46
  3.0 37.7 %all_to_all.25 = bf16[128,4,128]{2,1,0:T(4,128)(2,1)S(1)} all-to-all(bf16[128,4,128]{2,1,0:T(4,128)(2,1)S(1)} %shard_map.46), channel_id=1, replica_groups=mesh['y'=4,'z'=16,'core'=2,'run'=4] {'y','z','core'}, dimensions={0} | all-to-all | bytes 262144 | tf_op jit(solution)/shard_map/all_to_all | solution.py:140
  40.7 0.3 shard_map.47
  41.0 19.7 %all_to_all.26 = f32[32,40,128]{2,1,0:T(8,128)S(1)} all-to-all(f32[32,40,128]{2,1,0:T(8,128)S(1)} %bitcast.9), channel_id=1, replica_groups=mesh['y'=4,'z'=16,'core'=2,'run'=4] {'y','core','run'}, dimensions={0} | all-to-all | bytes 1310720 | tf_op jit(solution)/shard_map/all_to_all | solution.py:140
  60.7 0.1 reduce_sum.18
  60.8 17.8 %all_to_all.27 = f32[16,40,128]{2,1,0:T(8,128)S(1)} all-to-all(f32[16,40,128]{2,1,0:T(8,128)S(1)} %broadcast_in_dim.4), channel_id=1, replica_groups=mesh['y'=4,'z'=16,'core'=2,'run'=4] {'z'}, dimensions={0} | all-to-all | bytes 655360 | tf_op jit(solution)/shard_map/all_to_all | solution.py:140
  78.6 0.0 copy-start.1
  78.6 22.9 %all_to_all.28 = f32[32,40,128]{2,1,0:T(8,128)S(1)} all-to-all(f32[32,40,128]{2,1,0:T(8,128)S(1)} %broadcast_in_dim.5), channel_id=1, replica_groups=mesh['y'=4,'z'=16,'core'=2,'run'=4] {'y','core','run'}, dimensions={0} | all-to-all | bytes 1310720 | tf_op jit(solution)/shard_map/all_to_all | solution.py:140
  101.6 0.0 copy-done.1
  101.6 9.1 %shard_map.48 = f32[64,128]{1,0:T(8,128)S(1)} custom-call(f32[1280,128]{1,0:T(8,128)S(1)} %bitcast.8, f32[64,512]{1,0:T(8,128)S(1)} %bitcast.13, bf16[512,128]{1,0:T(8,128)(2,1)S(1)} %bitcast.11), custom_call_target="tpu_custom_call" | custom-call | tf_op jit(solution)/shard_map/pallas_call | solution.py:160
  110.6 20.8 %all_to_all.29 = f32[64,1,128]{2,1,0:T(1,128)S(1)} all-to-all(f32[64,1,128]{2,1,0:T(1,128)S(1)} %bitcast.14), channel_id=1, replica_groups=mesh['y'=4,'z'=16,'core'=2,'run'=4] {'y','z'}, dimensions={0} | all-to-all | bytes 65536 | tf_op jit(solution)/shard_map/all_to_all | solution.py:140
  131.4 0.9 shard_map.49
  (3 shorter events, 0.1 us)
Async XLA Ops:
  0.0 0.9 copy-start
  0.9 0.7 copy-start.2
  1.6 0.7 copy-start.3
  78.6 23.0 %copy-start.1 = (f32[512,64]{0,1:T(8,128)S(1)}, f32[512,64]{0,1:T(8,128)}, u32[]{:S(2)}) copy-start(f32[512,64]{0,1:T(8,128)} %param.7) | copy-start | bytes 393220

commit v3 on v2

--- a/solution.py
+++ b/solution.py
@@ -11,8 +11,9 @@
 HIGHEST = lax.Precision.HIGHEST
 VMEM = pl.BlockSpec(memory_space=pltpu.VMEM)
 SMEM = pl.BlockSpec(memory_space=pltpu.SMEM)
-FIB = ("y", "z", "core")
-PLANE = ("y", "core", "run")
+CHIPS = ("y", "pair", "side")
+FIB = CHIPS + ("core",)
+PLANE = ("y", "run", "side")
 PAIRS = [(i, j) for i in range(4) for j in range(i, 4)]
 
 
@@ -66,10 +67,16 @@
         out_ref[2 * chip + 1] = high.astype(jnp.bfloat16)
 
 
-def gram_kernel(fibres_ref, out_ref):
-    for at, (i, j) in enumerate(PAIRS):
-        out_ref[at * 128 : (at + 1) * 128, :] = nt(
-            fibres_ref[i * 128 : (i + 1) * 128, :], fibres_ref[j * 128 : (j + 1) * 128, :]
+def gram_kernel(own_ref, other_ref, out_ref):
+    core = lax.axis_index("core")
+    for at in range(len(PAIRS) // 2):
+        first, second = PAIRS[at], PAIRS[at + len(PAIRS) // 2]
+        i, j = (
+            pl.ds(pl.multiple_of(jnp.where(core == 0, low, high) * 128, 128), 128)
+            for low, high in zip(first, second)
+        )
+        out_ref[at * 128 : (at + 1) * 128, :] = nt(own_ref[i, :], own_ref[j, :]) + nt(
+            other_ref[i, :], other_ref[j, :]
         )
 
 
@@ -107,18 +114,22 @@
     return jnp.concatenate(rows, axis=0)
 
 
-def factor_kernel(packed_ref, start_ref, fibres_ref, out_ref, gram_ref):
+def factor_kernel(own_ref, other_ref, start_ref, fibres_ref, out_ref, gram_ref):
+    first = lax.axis_index("core") == 0
     for at, (i, j) in enumerate(PAIRS):
-        block = packed_ref[at * 128 : (at + 1) * 128, :]
+        rows = pl.ds(at % (len(PAIRS) // 2) * 128, 128)
+        mine = first if at < len(PAIRS) // 2 else jnp.logical_not(first)
+        block = jnp.where(mine, own_ref[rows, :], other_ref[rows, :])
         gram_ref[i * 128 : (i + 1) * 128, j * 128 : (j + 1) * 128] = block
         if i != j:
             gram_ref[j * 128 : (j + 1) * 128, i * 128 : (i + 1) * 128] = block.T
-    factor = start_ref[...]
-    for _ in range(ITERS):
-        product = nn(factor, gram_ref[...], HIGHEST)
+    product = nn(start_ref[...], gram_ref[...], HIGHEST)
+    for iteration in range(ITERS):
         small = nt(product, product, HIGHEST)
-        factor = nn(inverse_cholesky(small), product, HIGHEST)
-    core = nn(factor.astype(jnp.bfloat16), fibres_ref[...])
+        if iteration < ITERS - 1:
+            product = nn(product, gram_ref[...], HIGHEST)
+        product = nn(inverse_cholesky(small), product, HIGHEST)
+    core = nn(product.astype(jnp.bfloat16), fibres_ref[...])
     out_ref[...] = core.astype(jnp.bfloat16).astype(jnp.float32)
 
 
@@ -140,11 +151,16 @@
     return lax.all_to_all(array, axes, 0, 0, tiled=True)
 
 
+def to_other_core(array):
+    return lax.ppermute(array, "core", [(0, 1), (1, 0)])
+
+
 def sum_everywhere(packed):
-    rows = packed.shape[0] // 32
-    part = swap(packed.reshape(32, rows, LANES), PLANE).sum(0)
-    part = swap(jnp.broadcast_to(part[None], (16, rows, LANES)), "z").sum(0)
-    return swap(jnp.broadcast_to(part[None], (32, rows, LANES)), PLANE).reshape(packed.shape)
+    shards = 32
+    shard = (packed.shape[0] // shards // 4, 4, LANES)
+    part = swap(packed.reshape(shards, *shard), PLANE).sum(0)
+    part = swap(jnp.broadcast_to(part[None], (8, *shard)), "pair").sum(0)
+    return swap(jnp.broadcast_to(part[None], (shards, *shard)), PLANE).reshape(packed.shape)
 
 
 def per_device(slab, chord_weight, span_weight, start):
@@ -154,22 +170,24 @@
         slab, chord_weight, span_weight
     )
     fibres = swap(send, FIB).reshape(tiles * rows, LANES)
-    packed = call(gram_kernel, (len(PAIRS) * 128, 128), jnp.float32, [VMEM])(fibres)
-    packed = sum_everywhere(packed)
+    half = call(gram_kernel, (len(PAIRS) // 2 * 128, 128), jnp.float32, [VMEM] * 2)(
+        fibres, to_other_core(fibres)
+    )
+    half = sum_everywhere(half)
     chords, rank = start.shape
     parts = call(
         factor_kernel,
         (rank, LANES),
         jnp.float32,
-        [VMEM] * 3,
+        [VMEM] * 4,
         [pltpu.VMEM((chords, chords), jnp.float32)],
-    )(packed, start.T, fibres)
-    parts = swap(parts.reshape(rank, 1, LANES), ("y", "z")).reshape(rank, LANES)
+    )(half, to_other_core(half), start.T, fibres)
+    parts = swap(parts.reshape(rank, 1, LANES), CHIPS).reshape(rank, LANES)
     return call(unfold_kernel, (1, K // 2, 4 * rank), jnp.bfloat16, [VMEM])(parts)
 
 
 def solution(mesh):
-    fine = Mesh(mesh.devices.reshape(4, 16, 2, 4), FIB + ("run",))
+    fine = Mesh(mesh.devices.reshape(4, 8, 2, 2, 4), FIB + ("run",))
     return jax.shard_map(
         per_device,
         mesh=fine,

time: 133 us -> 121 us (0.910)
  blocking collectives: 119 us -> 96.6 us
  starting transfers between devices: 0 us -> 9.76 us
  waiting for transfers between devices: 0 us -> 2.2 us
    all_to_all x5, blocking collectives: 119 us -> 96.6 us  [swap(): return lax.all_to_all(array, axes, 0, 0, tiled=True)]
    ppermute x0 -> x2, starting transfers between devices: none -> 9.76 us  [to_other_core(): return lax.ppermute(array, 'core', [(0, 1), (1, 0)])]
    ppermute x0 -> x2, waiting for transfers between devices: none -> 2.2 us  [to_other_core(): return lax.ppermute(array, 'core', [(0, 1), (1, 0)])]
  transfers between devices with their start and end apart: 0 -> 2, of which waited for: 0 -> 2; matrix products, arithmetic and copies ran while one was open for 0% -> 0% of each run, Pallas kernels for 0% -> 0%
where the time goes in v3:
time: 121 us
  blocking collectives  96.6 us (80%)
  Pallas kernels  10.1 us (8%)
  starting transfers between devices  9.76 us (8%)
  local copies, waits for them, and re-layouts  2.3 us (2%)
  waiting for transfers between devices  2.2 us (2%)
    all_to_all x5, blocking collectives, swap(): return lax.all_to_all(array, axes, 0, 0, tiled=True)  96.6 us
    ppermute x2, starting transfers between devices, to_other_core(): return lax.ppermute(array, 'core', [(0, 1), (1, 0)])  9.76 us
    pallas_call x1, Pallas kernels, per_device(): call(factor_kernel, (rank, LANES), jnp.float32, [VMEM] * 4, [pltpu.VMEM((...  8.17 us
  transfers between devices with their start and end apart: 2, of which 2 were waited for; matrix products, arithmetic and copies ran while one was open for 0% of the time, Pallas kernels for 0%

profile of v3, /device:TPU:1, one launch (start us, length us, event | category | flops | bytes accessed | tf_op | source)
XLA Modules:
  0.0 121.1 jit_solution(3397124050181196485)
XLA Ops:
  0.0 0.0 copy-start
  0.0 0.9 copy-done
  0.9 0.0 copy-start.2
  0.9 0.7 copy-done.2
  1.6 0.0 copy-start.3
  1.6 0.7 copy-done.3
  2.2 0.7 shard_map.46
  3.0 37.7 %all_to_all.25 = bf16[128,4,128]{2,1,0:T(4,128)(2,1)S(1)} all-to-all(bf16[128,4,128]{2,1,0:T(4,128)(2,1)S(1)} %shard_map.46), channel_id=1, replica_groups=mesh['y'=4,'pair'=8,'side'=2,'core'=2,'run'=4] {'y','pair','side','core'}, dimensions={0} | all-to-all | bytes 262144 | tf_op jit(solution)/shard_map/all_to_all | solution.py:151
  40.7 3.7 %collective-permute-start = (bf16[512,128]{1,0:T(8,128)(2,1)S(1)}, bf16[512,128]{1,0:T(8,128)(2,1)S(1)}, u32[]{:S(2)}, u32[]{:S(2)}) collective-permute-start(bf16[512,128]{1,0:T(8,128)(2,1)S(1)} %bitcast.11), channel_id=1, source_target_pairs={{0,4},{4,0},{1,5},{5,1},{2,6},{6,2},{3,7},{7,3},{8,12},{12,8},{9,1... | collective-permute-start | bytes 393224 | tf_op jit(solution)/shard_map/ppermute | solution.py:155
  44.4 1.0 collective-permute-done.other_ref
  45.4 0.4 shard_map.47
  45.7 14.9 %all_to_all.26 = f32[32,5,4,128]{3,2,1,0:T(4,128)S(1)} all-to-all(f32[32,5,4,128]{3,2,1,0:T(4,128)S(1)} %bitcast.8), channel_id=1, replica_groups=mesh['y'=4,'pair'=8,'side'=2,'core'=2,'run'=4] {'y','run','side'}, dimensions={0} | all-to-all | bytes 655360 | tf_op jit(solution)/shard_map/all_to_all | solution.py:151
  60.7 0.1 reduce_sum.18
  60.7 14.6 %all_to_all.27 = f32[8,5,4,128]{3,2,1,0:T(4,128)S(1)} all-to-all(f32[8,5,4,128]{3,2,1,0:T(4,128)S(1)} %broadcast_in_dim.4), channel_id=1, replica_groups=mesh['y'=4,'pair'=8,'side'=2,'core'=2,'run'=4] {'pair'}, dimensions={0} | all-to-all | bytes 163840 | tf_op jit(solution)/shard_map/all_to_all | solution.py:151
  75.4 0.0 copy-start.1
  75.4 12.3 %all_to_all.28 = f32[32,5,4,128]{3,2,1,0:T(4,128)S(1)} all-to-all(f32[32,5,4,128]{3,2,1,0:T(4,128)S(1)} %broadcast_in_dim.5), channel_id=1, replica_groups=mesh['y'=4,'pair'=8,'side'=2,'core'=2,'run'=4] {'y','run','side'}, dimensions={0} | all-to-all | bytes 655360 | tf_op jit(solution)/shard_map/all_to_all | solution.py:151
  87.7 6.0 %collective-permute-start.1 = (f32[640,128]{1,0:T(8,128)S(1)}, f32[640,128]{1,0:T(8,128)S(1)}, u32[]{:S(2)}, u32[]{:S(2)}) collective-permute-start(f32[640,128]{1,0:T(8,128)S(1)} %bitcast.9), channel_id=1, source_target_pairs={{0,4},{4,0},{1,5},{5,1},{2,6},{6,2},{3,7},{7,3},{8,12},{12,8},{9,1... | collective-permute-start | bytes 983048 | tf_op jit(solution)/shard_map/ppermute | solution.py:155
  93.7 1.2 %collective-permute-done.1.other_ref = f32[640,128]{1,0:T(8,128)S(1)} collective-permute-done((f32[640,128]{1,0:T(8,128)S(1)}, f32[640,128]{1,0:T(8,128)S(1)}, u32[]{:S(2)}, u32[]{:S(2)}) %collective-permute-start.1) | collective-permute-done | bytes 327712 | tf_op jit(solution)/shard_map/ppermute | solution.py:155
  95.0 0.0 copy-done.1
  95.0 8.2 %shard_map.48 = f32[64,128]{1,0:T(8,128)S(1)} custom-call(f32[640,128]{1,0:T(8,128)S(1)} %bitcast.10, f32[640,128]{1,0:T(8,128)S(1)} %collective-permute-done.1.other_ref, f32[64,512]{1,0:T(8,128)S(1)} %bitcast.15, bf16[512,128]{1,0:T(8,128)(2,1)S(1)} %bitcast.13), custom_call_target="tpu_custom_call" | custom-call | tf_op jit(solution)/shard_map/pallas_call | solution.py:178
  103.1 17.1 %all_to_all.29 = f32[64,1,128]{2,1,0:T(1,128)S(1)} all-to-all(f32[64,1,128]{2,1,0:T(1,128)S(1)} %bitcast.16), channel_id=1, replica_groups=mesh['y'=4,'pair'=8,'side'=2,'core'=2,'run'=4] {'y','pair','side'}, dimensions={0} | all-to-all | bytes 65536 | tf_op jit(solution)/shard_map/all_to_all | solution.py:151
  120.2 0.9 shard_map.49
  (3 shorter events, 0.1 us)
Async XLA Ops:
  0.0 0.9 copy-start
  0.9 0.7 copy-start.2
  1.6 0.7 copy-start.3
  40.7 4.7 %collective-permute-start = (bf16[512,128]{1,0:T(8,128)(2,1)S(1)}, bf16[512,128]{1,0:T(8,128)(2,1)S(1)}, u32[]{:S(2)}, u32[]{:S(2)}) collective-permute-start(bf16[512,128]{1,0:T(8,128)(2,1)S(1)} %bitcast.11), channel_id=1, source_target_pairs={{0,4},{4,0},{1,5},{5,1},{2,6},{6,2},{3,7},{7,3},{8,12},{12,8},{9,1... | collective-permute-start | bytes 393224 | tf_op jit(solution)/shard_map/ppermute | solution.py:155
  75.4 19.6 %copy-start.1 = (f32[512,64]{0,1:T(8,128)S(1)}, f32[512,64]{0,1:T(8,128)}, u32[]{:S(2)}) copy-start(f32[512,64]{0,1:T(8,128)} %param.7) | copy-start | bytes 393220
  87.7 7.3 %collective-permute-start.1 = (f32[640,128]{1,0:T(8,128)S(1)}, f32[640,128]{1,0:T(8,128)S(1)}, u32[]{:S(2)}, u32[]{:S(2)}) collective-permute-start(f32[640,128]{1,0:T(8,128)S(1)} %bitcast.9), channel_id=1, source_target_pairs={{0,4},{4,0},{1,5},{5,1},{2,6},{6,2},{3,7},{7,3},{8,12},{12,8},{9,1... | collective-permute-start | bytes 983048 | tf_op jit(solution)/shard_map/ppermute | solution.py:155

commit v4 on v3

--- a/solution.py
+++ b/solution.py
@@ -12,9 +12,8 @@
 VMEM = pl.BlockSpec(memory_space=pltpu.VMEM)
 SMEM = pl.BlockSpec(memory_space=pltpu.SMEM)
 CHIPS = ("y", "pair", "side")
-FIB = CHIPS + ("core",)
 PLANE = ("y", "run", "side")
-PAIRS = [(i, j) for i in range(4) for j in range(i, 4)]
+PAIRS = [(0, 0), (0, 1), (1, 1), (0, 2), (1, 3), (2, 2), (2, 3), (3, 3), (2, 1), (3, 0)]
 
 
 def call(kernel, shape, dtype, specs, scratch=()):
@@ -68,16 +67,20 @@
 
 
 def gram_kernel(own_ref, other_ref, out_ref):
-    core = lax.axis_index("core")
-    for at in range(len(PAIRS) // 2):
-        first, second = PAIRS[at], PAIRS[at + len(PAIRS) // 2]
-        i, j = (
-            pl.ds(pl.multiple_of(jnp.where(core == 0, low, high) * 128, 128), 128)
-            for low, high in zip(first, second)
-        )
-        out_ref[at * 128 : (at + 1) * 128, :] = nt(own_ref[i, :], own_ref[j, :]) + nt(
-            other_ref[i, :], other_ref[j, :]
-        )
+    first = lax.axis_index("core") == 0
+    crossed = [(0, 2), (1, 3)]
+    for at, (i, j) in enumerate([(0, 0), (0, 1), (1, 1), *crossed]):
+        total = None
+        for part in range(2):
+            left = own_ref[part, i * 128 : (i + 1) * 128, :]
+            if j < 2:
+                right = own_ref[part, j * 128 : (j + 1) * 128, :]
+            else:
+                low, high = other_ref[part, :128, :], other_ref[part, 128:, :]
+                right = jnp.where(first == (j == 2), low, high)
+            term = nt(left, right)
+            total = term if total is None else total + term
+        out_ref[at * 128 : (at + 1) * 128, :] = total
 
 
 def inverse_cholesky(small):
@@ -114,23 +117,39 @@
     return jnp.concatenate(rows, axis=0)
 
 
-def factor_kernel(own_ref, other_ref, start_ref, fibres_ref, out_ref, gram_ref):
-    first = lax.axis_index("core") == 0
+def factor_kernel(own_ref, other_ref, start_ref, own_fibres_ref, other_fibres_ref, out_ref, gram_ref):
+    core = lax.axis_index("core")
     for at, (i, j) in enumerate(PAIRS):
-        rows = pl.ds(at % (len(PAIRS) // 2) * 128, 128)
-        mine = first if at < len(PAIRS) // 2 else jnp.logical_not(first)
+        rows = pl.ds(at % 5 * 128, 128)
+        mine = core == at // 5
         block = jnp.where(mine, own_ref[rows, :], other_ref[rows, :])
         gram_ref[i * 128 : (i + 1) * 128, j * 128 : (j + 1) * 128] = block
         if i != j:
             gram_ref[j * 128 : (j + 1) * 128, i * 128 : (i + 1) * 128] = block.T
-    product = nn(start_ref[...], gram_ref[...], HIGHEST)
+    chords = gram_ref.shape[0]
+    source = lax.broadcasted_iota(jnp.int32, (chords, chords), 0)
+    target = lax.broadcasted_iota(jnp.int32, (chords, chords), 1)
+    half = chords // 2
+    wanted = target % half // 4 * 8 + target // half * 4 + target % 4
+    order = (source == wanted).astype(jnp.bfloat16)
+    rest = start_ref[...]
+    start = jnp.zeros_like(rest)
+    for _ in range(3):
+        part = rest.astype(jnp.bfloat16)
+        rest = rest - part.astype(jnp.float32)
+        start = start + nn(part, order)
+    product = nn(start, gram_ref[...], HIGHEST)
     for iteration in range(ITERS):
         small = nt(product, product, HIGHEST)
         if iteration < ITERS - 1:
             product = nn(product, gram_ref[...], HIGHEST)
         product = nn(inverse_cholesky(small), product, HIGHEST)
-    core = nn(product.astype(jnp.bfloat16), fibres_ref[...])
-    out_ref[...] = core.astype(jnp.bfloat16).astype(jnp.float32)
+    narrow = product.astype(jnp.bfloat16)
+    own = jnp.where(core == 0, own_fibres_ref[0], own_fibres_ref[1])
+    other = jnp.where(core == 0, other_fibres_ref[0], other_fibres_ref[1])
+    low, high = jnp.where(core == 0, own, other), jnp.where(core == 0, other, own)
+    ranked = nn(narrow[:, :half], low) + nn(narrow[:, half:], high)
+    out_ref[...] = ranked.astype(jnp.bfloat16).astype(jnp.float32)
 
 
 def unfold_kernel(parts_ref, out_ref):
@@ -169,29 +188,30 @@
     send = call(weigh_kernel, (tiles, rows, LANES), jnp.bfloat16, [VMEM, SMEM, SMEM])(
         slab, chord_weight, span_weight
     )
-    fibres = swap(send, FIB).reshape(tiles * rows, LANES)
-    half = call(gram_kernel, (len(PAIRS) // 2 * 128, 128), jnp.float32, [VMEM] * 2)(
-        fibres, to_other_core(fibres)
-    )
+    chips = tiles // 2
+    received = swap(send.reshape(chips, 2, rows, LANES), CHIPS)
+    own = received.transpose(1, 0, 2, 3).reshape(2, chips * rows, LANES)
+    other = to_other_core(own)
+    half = call(gram_kernel, (len(PAIRS) // 2 * 128, 128), jnp.float32, [VMEM] * 2)(own, other)
     half = sum_everywhere(half)
     chords, rank = start.shape
     parts = call(
         factor_kernel,
         (rank, LANES),
         jnp.float32,
-        [VMEM] * 4,
+        [VMEM] * 5,
         [pltpu.VMEM((chords, chords), jnp.float32)],
-    )(half, to_other_core(half), start.T, fibres)
+    )(half, to_other_core(half), start.T, own, other)
     parts = swap(parts.reshape(rank, 1, LANES), CHIPS).reshape(rank, LANES)
     return call(unfold_kernel, (1, K // 2, 4 * rank), jnp.bfloat16, [VMEM])(parts)
 
 
 def solution(mesh):
-    fine = Mesh(mesh.devices.reshape(4, 8, 2, 2, 4), FIB + ("run",))
+    fine = Mesh(mesh.devices.reshape(4, 8, 2, 2, 4), CHIPS + ("core", "run"))
     return jax.shard_map(
         per_device,
         mesh=fine,
-        in_specs=(P("run", FIB, None), P(FIB), P(), P()),
-        out_specs=P("run", FIB, None),
+        in_specs=(P("run", CHIPS + ("core",), None), P(CHIPS + ("core",)), P(), P()),
+        out_specs=P("run", CHIPS + ("core",), None),
         check_vma=False,
     )

time: 121 us -> 120 us (level)
  blocking collectives: 96.6 us -> 93.2 us
  starting transfers between devices: 9.76 us -> 11.7 us
    all_to_all x5, blocking collectives: 96.6 us -> 93.2 us  [swap(): return lax.all_to_all(array, axes, 0, 0, tiled=True)]
    ppermute x2, starting transfers between devices: 9.76 us -> 11.7 us  [to_other_core(): return lax.ppermute(array, 'core', [(0, 1), (1, 0)])]
where the time goes in v4:
time: 120 us
  blocking collectives  93.2 us (78%)
  starting transfers between devices  11.7 us (10%)
  Pallas kernels  10.5 us (9%)
  local copies, waits for them, and re-layouts  2.35 us (2%)
  waiting for transfers between devices  2.2 us (2%)
    all_to_all x5, blocking collectives, swap(): return lax.all_to_all(array, axes, 0, 0, tiled=True)  93.2 us
    ppermute x2, starting transfers between devices, to_other_core(): return lax.ppermute(array, 'core', [(0, 1), (1, 0)])  11.7 us
    pallas_call x1, Pallas kernels, per_device(): call(factor_kernel, (rank, LANES), jnp.float32, [VMEM] * 5, [pltpu.VMEM((...  8.54 us
  transfers between devices with their start and end apart: 2, of which 2 were waited for; matrix products, arithmetic and copies ran while one was open for 0% of the time, Pallas kernels for 0%

profile of v4, /device:TPU:1, one launch (start us, length us, event | category | flops | bytes accessed | tf_op | source)
XLA Modules:
  0.0 120.1 jit_solution(16454991125749487381)
XLA Ops:
  0.0 0.0 copy-start.1
  0.0 0.9 copy-done.1
  0.9 0.0 copy-start.2
  0.9 0.7 copy-done.2
  1.6 0.0 copy-start.3
  1.6 0.7 copy-done.3
  2.2 0.7 shard_map.46
  3.0 33.0 %all_to_all.25 = bf16[64,2,4,128]{3,2,1,0:T(4,128)(2,1)S(1)} all-to-all(bf16[64,2,4,128]{3,2,1,0:T(4,128)(2,1)S(1)} %bitcast.16), channel_id=1, replica_groups=mesh['y'=4,'pair'=8,'side'=2,'core'=2,'run'=4] {'y','pair','side'}, dimensions={0} | all-to-all | bytes 262144 | tf_op jit(solution)/shard_map/all_to_all | solution.py:170
  36.1 5.2 %collective-permute-start = (bf16[2,256,128]{2,1,0:T(8,128)(2,1)S(1)}, bf16[2,256,128]{2,1,0:T(8,128)(2,1)S(1)}, u32[]{:S(2)}, u32[]{:S(2)}) collective-permute-start(bf16[2,256,128]{2,1,0:T(8,128)(2,1)S(1)} %bitcast.13), channel_id=1, source_target_pairs={{0,4},{4,0},{1,5},{5,1},{2,6},{6,2},{3,7},{7,3},{8,12},{12,8},{9,1... | collective-permute-start | bytes 393224 | tf_op jit(solution)/shard_map/ppermute | solution.py:174
  41.3 1.0 collective-permute-done.other_ref.other_fibres_ref
  42.3 0.3 shard_map.47
  42.6 15.8 %all_to_all.26 = f32[32,5,4,128]{3,2,1,0:T(4,128)S(1)} all-to-all(f32[32,5,4,128]{3,2,1,0:T(4,128)S(1)} %bitcast.12), channel_id=1, replica_groups=mesh['y'=4,'pair'=8,'side'=2,'core'=2,'run'=4] {'y','run','side'}, dimensions={0} | all-to-all | bytes 655360 | tf_op jit(solution)/shard_map/all_to_all | solution.py:170
  58.5 0.1 reduce_sum.18
  58.6 15.1 %all_to_all.27 = f32[8,5,4,128]{3,2,1,0:T(4,128)S(1)} all-to-all(f32[8,5,4,128]{3,2,1,0:T(4,128)S(1)} %broadcast_in_dim.4), channel_id=1, replica_groups=mesh['y'=4,'pair'=8,'side'=2,'core'=2,'run'=4] {'pair'}, dimensions={0} | all-to-all | bytes 163840 | tf_op jit(solution)/shard_map/all_to_all | solution.py:170
  73.8 0.0 copy-start
  73.8 12.1 %all_to_all.28 = f32[32,5,4,128]{3,2,1,0:T(4,128)S(1)} all-to-all(f32[32,5,4,128]{3,2,1,0:T(4,128)S(1)} %broadcast_in_dim.5), channel_id=1, replica_groups=mesh['y'=4,'pair'=8,'side'=2,'core'=2,'run'=4] {'y','run','side'}, dimensions={0} | all-to-all | bytes 655360 | tf_op jit(solution)/shard_map/all_to_all | solution.py:170
  85.8 6.5 %collective-permute-start.1 = (f32[640,128]{1,0:T(8,128)S(1)}, f32[640,128]{1,0:T(8,128)S(1)}, u32[]{:S(2)}, u32[]{:S(2)}) collective-permute-start(f32[640,128]{1,0:T(8,128)S(1)} %bitcast.10), channel_id=1, source_target_pairs={{0,4},{4,0},{1,5},{5,1},{2,6},{6,2},{3,7},{7,3},{8,12},{12,8},{9,1... | collective-permute-start | bytes 983048 | tf_op jit(solution)/shard_map/ppermute | solution.py:174
  92.3 1.2 %collective-permute-done.1.other_ref = f32[640,128]{1,0:T(8,128)S(1)} collective-permute-done((f32[640,128]{1,0:T(8,128)S(1)}, f32[640,128]{1,0:T(8,128)S(1)}, u32[]{:S(2)}, u32[]{:S(2)}) %collective-permute-start.1) | collective-permute-done | bytes 327712 | tf_op jit(solution)/shard_map/ppermute | solution.py:174
  93.6 0.0 copy-done
  93.6 8.5 %shard_map.48 = f32[64,128]{1,0:T(8,128)S(1)} custom-call(f32[640,128]{1,0:T(8,128)S(1)} %bitcast.11, f32[640,128]{1,0:T(8,128)S(1)} %collective-permute-done.1.other_ref, f32[64,512]{1,0:T(8,128)S(1)} %bitcast.17, bf16[2,256,128]{2,1,0:T(8,128)(2,1)S(1)} %bitcast.15, bf16[2,256,128]{2,1,0:T(8,128)(2,1)S(1)} %collective-permute-done.other_ref.other_fibres_ref), custom_call_target="tpu_custom_call" | custom-call | tf_op jit(solution)/shard_map/pallas_call | solution.py:198
  102.1 17.1 %all_to_all.29 = f32[64,1,128]{2,1,0:T(1,128)S(1)} all-to-all(f32[64,1,128]{2,1,0:T(1,128)S(1)} %bitcast.18), channel_id=1, replica_groups=mesh['y'=4,'pair'=8,'side'=2,'core'=2,'run'=4] {'y','pair','side'}, dimensions={0} | all-to-all | bytes 65536 | tf_op jit(solution)/shard_map/all_to_all | solution.py:170
  119.2 0.9 shard_map.49
  (4 shorter events, 0.1 us)
Async XLA Ops:
  0.0 0.9 copy-start.1
  0.9 0.7 copy-start.2
  1.6 0.7 copy-start.3
  36.1 6.2 %collective-permute-start = (bf16[2,256,128]{2,1,0:T(8,128)(2,1)S(1)}, bf16[2,256,128]{2,1,0:T(8,128)(2,1)S(1)}, u32[]{:S(2)}, u32[]{:S(2)}) collective-permute-start(bf16[2,256,128]{2,1,0:T(8,128)(2,1)S(1)} %bitcast.13), channel_id=1, source_target_pairs={{0,4},{4,0},{1,5},{5,1},{2,6},{6,2},{3,7},{7,3},{8,12},{12,8},{9,1... | collective-permute-start | bytes 393224 | tf_op jit(solution)/shard_map/ppermute | solution.py:174
  73.8 19.8 %copy-start = (f32[512,64]{0,1:T(8,128)S(1)}, f32[512,64]{0,1:T(8,128)}, u32[]{:S(2)}) copy-start(f32[512,64]{0,1:T(8,128)} %param.7) | copy-start | bytes 393220
  85.8 7.7 %collective-permute-start.1 = (f32[640,128]{1,0:T(8,128)S(1)}, f32[640,128]{1,0:T(8,128)S(1)}, u32[]{:S(2)}, u32[]{:S(2)}) collective-permute-start(f32[640,128]{1,0:T(8,128)S(1)} %bitcast.10), channel_id=1, source_target_pairs={{0,4},{4,0},{1,5},{5,1},{2,6},{6,2},{3,7},{7,3},{8,12},{12,8},{9,1... | collective-permute-start | bytes 983048 | tf_op jit(solution)/shard_map/ppermute | solution.py:174

commit v5 on v4

--- a/solution.py
+++ b/solution.py
@@ -10,7 +10,7 @@
 LANES = 128
 HIGHEST = lax.Precision.HIGHEST
 VMEM = pl.BlockSpec(memory_space=pltpu.VMEM)
-SMEM = pl.BlockSpec(memory_space=pltpu.SMEM)
+HBM = pl.BlockSpec(memory_space=pltpu.HBM)
 CHIPS = ("y", "pair", "side")
 PLANE = ("y", "run", "side")
 PAIRS = [(0, 0), (0, 1), (1, 1), (0, 2), (1, 3), (2, 2), (2, 3), (3, 3), (2, 1), (3, 0)]
@@ -45,7 +45,16 @@
     )
 
 
-def weigh_kernel(slab_ref, chord_ref, span_ref, out_ref):
+def weigh_kernel(slab_hbm, chord_hbm, span_hbm, out_ref, slab_ref, chord_ref, span_ref, sems):
+    copies = [
+        pltpu.make_async_copy(slab_hbm, slab_ref, sems.at[0]),
+        pltpu.make_async_copy(chord_hbm, chord_ref, sems.at[1]),
+        pltpu.make_async_copy(span_hbm, span_ref, sems.at[2]),
+    ]
+    for copy in copies:
+        copy.start()
+    for copy in copies[::-1]:
+        copy.wait()
     lane = lax.broadcasted_iota(jnp.int32, (1, LANES), 1)
     row = lax.broadcasted_iota(jnp.int32, (out_ref.shape[1], LANES), 0)
     chord = jnp.zeros(row.shape, jnp.float32)
@@ -117,16 +126,8 @@
     return jnp.concatenate(rows, axis=0)
 
 
-def factor_kernel(own_ref, other_ref, start_ref, own_fibres_ref, other_fibres_ref, out_ref, gram_ref):
-    core = lax.axis_index("core")
-    for at, (i, j) in enumerate(PAIRS):
-        rows = pl.ds(at % 5 * 128, 128)
-        mine = core == at // 5
-        block = jnp.where(mine, own_ref[rows, :], other_ref[rows, :])
-        gram_ref[i * 128 : (i + 1) * 128, j * 128 : (j + 1) * 128] = block
-        if i != j:
-            gram_ref[j * 128 : (j + 1) * 128, i * 128 : (i + 1) * 128] = block.T
-    chords = gram_ref.shape[0]
+def order_kernel(start_ref, out_ref):
+    chords = start_ref.shape[1]
     source = lax.broadcasted_iota(jnp.int32, (chords, chords), 0)
     target = lax.broadcasted_iota(jnp.int32, (chords, chords), 1)
     half = chords // 2
@@ -138,12 +139,25 @@
         part = rest.astype(jnp.bfloat16)
         rest = rest - part.astype(jnp.float32)
         start = start + nn(part, order)
-    product = nn(start, gram_ref[...], HIGHEST)
+    out_ref[...] = start
+
+
+def factor_kernel(own_ref, other_ref, start_ref, own_fibres_ref, other_fibres_ref, out_ref, gram_ref):
+    core = lax.axis_index("core")
+    for at, (i, j) in enumerate(PAIRS):
+        rows = pl.ds(at % 5 * 128, 128)
+        mine = core == at // 5
+        block = jnp.where(mine, own_ref[rows, :], other_ref[rows, :])
+        gram_ref[i * 128 : (i + 1) * 128, j * 128 : (j + 1) * 128] = block
+        if i != j:
+            gram_ref[j * 128 : (j + 1) * 128, i * 128 : (i + 1) * 128] = block.T
+    product = nn(start_ref[...], gram_ref[...], HIGHEST)
     for iteration in range(ITERS):
         small = nt(product, product, HIGHEST)
         if iteration < ITERS - 1:
             product = nn(product, gram_ref[...], HIGHEST)
         product = nn(inverse_cholesky(small), product, HIGHEST)
+    half = gram_ref.shape[0] // 2
     narrow = product.astype(jnp.bfloat16)
     own = jnp.where(core == 0, own_fibres_ref[0], own_fibres_ref[1])
     other = jnp.where(core == 0, other_fibres_ref[0], other_fibres_ref[1])
@@ -185,23 +199,31 @@
 def per_device(slab, chord_weight, span_weight, start):
     rows, columns = slab.shape[1:]
     tiles = columns // LANES
-    send = call(weigh_kernel, (tiles, rows, LANES), jnp.bfloat16, [VMEM, SMEM, SMEM])(
-        slab, chord_weight, span_weight
+    inputs = slab, chord_weight, span_weight
+    scratch = [
+        pltpu.VMEM(slab.shape, slab.dtype),
+        pltpu.SMEM(chord_weight.shape, jnp.float32),
+        pltpu.SMEM(span_weight.shape, jnp.float32),
+        pltpu.SemaphoreType.DMA((3,)),
+    ]
+    send = call(weigh_kernel, (tiles, rows, LANES), jnp.bfloat16, [HBM] * 3, scratch)(
+        *(pltpu.with_memory_space_constraint(array, pltpu.HBM) for array in inputs)
     )
     chips = tiles // 2
     received = swap(send.reshape(chips, 2, rows, LANES), CHIPS)
     own = received.transpose(1, 0, 2, 3).reshape(2, chips * rows, LANES)
     other = to_other_core(own)
+    chords, rank = start.shape
+    ordered = call(order_kernel, (rank, chords), jnp.float32, [VMEM])(start.T)
     half = call(gram_kernel, (len(PAIRS) // 2 * 128, 128), jnp.float32, [VMEM] * 2)(own, other)
     half = sum_everywhere(half)
-    chords, rank = start.shape
     parts = call(
         factor_kernel,
         (rank, LANES),
         jnp.float32,
         [VMEM] * 5,
         [pltpu.VMEM((chords, chords), jnp.float32)],
-    )(half, to_other_core(half), start.T, own, other)
+    )(half, to_other_core(half), ordered, own, other)
     parts = swap(parts.reshape(rank, 1, LANES), CHIPS).reshape(rank, LANES)
     return call(unfold_kernel, (1, K // 2, 4 * rank), jnp.bfloat16, [VMEM])(parts)
 

time: 120 us -> 118 us (0.983)
  local copies, waits for them, and re-layouts: 2.35 us -> 0.11 us
    unnamed x8 -> x2, local copies, waits for them, and re-layouts: 2.24 us -> 0.01 us
where the time goes in v5:
time: 118 us
  blocking collectives  93.2 us (79%)
  starting transfers between devices  11.7 us (10%)
  Pallas kernels  11 us (9%)
  waiting for transfers between devices  1.76 us (1%)
    all_to_all x5, blocking collectives, swap(): return lax.all_to_all(array, axes, 0, 0, tiled=True)  93.2 us
    ppermute x2, starting transfers between devices, to_other_core(): return lax.ppermute(array, 'core', [(0, 1), (1, 0)])  11.7 us
    pallas_call x1, Pallas kernels, per_device(): call(factor_kernel, (rank, LANES), jnp.float32, [VMEM] * 5, [pltpu.VMEM((...  8.27 us
  transfers between devices with their start and end apart: 2, of which 2 were waited for; matrix products, arithmetic and copies ran while one was open for 0% of the time, Pallas kernels for 0%

profile of v5, /device:TPU:1, one launch (start us, length us, event | category | flops | bytes accessed | tf_op | source)
XLA Modules:
  0.0 117.9 jit_solution(8710266643238974260)
XLA Ops:
  0.0 1.1 shard_map.46
  1.1 33.0 %all_to_all.25 = bf16[64,2,4,128]{3,2,1,0:T(4,128)(2,1)S(1)} all-to-all(bf16[64,2,4,128]{3,2,1,0:T(4,128)(2,1)S(1)} %bitcast.16), channel_id=1, replica_groups=mesh['y'=4,'pair'=8,'side'=2,'core'=2,'run'=4] {'y','pair','side'}, dimensions={0} | all-to-all | bytes 262144 | tf_op jit(solution)/shard_map/all_to_all | solution.py:184
  34.2 5.2 %collective-permute-start = (bf16[2,256,128]{2,1,0:T(8,128)(2,1)S(1)}, bf16[2,256,128]{2,1,0:T(8,128)(2,1)S(1)}, u32[]{:S(2)}, u32[]{:S(2)}) collective-permute-start(bf16[2,256,128]{2,1,0:T(8,128)(2,1)S(1)} %bitcast.13), channel_id=1, source_target_pairs={{0,4},{4,0},{1,5},{5,1},{2,6},{6,2},{3,7},{7,3},{8,12},{12,8},{9,1... | collective-permute-start | bytes 393224 | tf_op jit(solution)/shard_map/ppermute | solution.py:188
  39.5 1.0 collective-permute-done.other_ref.other_fibres_ref
  40.4 0.3 shard_map.47
  40.8 15.8 %all_to_all.26 = f32[32,5,4,128]{3,2,1,0:T(4,128)S(1)} all-to-all(f32[32,5,4,128]{3,2,1,0:T(4,128)S(1)} %bitcast.12), channel_id=1, replica_groups=mesh['y'=4,'pair'=8,'side'=2,'core'=2,'run'=4] {'y','run','side'}, dimensions={0} | all-to-all | bytes 655360 | tf_op jit(solution)/shard_map/all_to_all | solution.py:184
  56.6 0.1 reduce_sum.18
  56.7 15.1 %all_to_all.27 = f32[8,5,4,128]{3,2,1,0:T(4,128)S(1)} all-to-all(f32[8,5,4,128]{3,2,1,0:T(4,128)S(1)} %broadcast_in_dim.4), channel_id=1, replica_groups=mesh['y'=4,'pair'=8,'side'=2,'core'=2,'run'=4] {'pair'}, dimensions={0} | all-to-all | bytes 163840 | tf_op jit(solution)/shard_map/all_to_all | solution.py:184
  71.9 0.0 copy-start
  71.9 12.1 %all_to_all.28 = f32[32,5,4,128]{3,2,1,0:T(4,128)S(1)} all-to-all(f32[32,5,4,128]{3,2,1,0:T(4,128)S(1)} %broadcast_in_dim.5), channel_id=1, replica_groups=mesh['y'=4,'pair'=8,'side'=2,'core'=2,'run'=4] {'y','run','side'}, dimensions={0} | all-to-all | bytes 655360 | tf_op jit(solution)/shard_map/all_to_all | solution.py:184
  84.0 6.5 %collective-permute-start.1 = (f32[640,128]{1,0:T(8,128)S(1)}, f32[640,128]{1,0:T(8,128)S(1)}, u32[]{:S(2)}, u32[]{:S(2)}) collective-permute-start(f32[640,128]{1,0:T(8,128)S(1)} %bitcast.10), channel_id=1, source_target_pairs={{0,4},{4,0},{1,5},{5,1},{2,6},{6,2},{3,7},{7,3},{8,12},{12,8},{9,1... | collective-permute-start | bytes 983048 | tf_op jit(solution)/shard_map/ppermute | solution.py:188
  90.5 0.0 copy-done
  90.5 0.4 shard_map.48.start_ref
  90.9 0.8 collective-permute-done.1.other_ref
  91.7 8.3 %shard_map.49 = f32[64,128]{1,0:T(8,128)S(1)} custom-call(f32[640,128]{1,0:T(8,128)S(1)} %bitcast.11, f32[640,128]{1,0:T(8,128)S(1)} %collective-permute-done.1.other_ref, f32[64,512]{1,0:T(8,128)S(1)} %shard_map.48.start_ref, bf16[2,256,128]{2,1,0:T(8,128)(2,1)S(1)} %bitcast.15, bf16[2,256,128]{2,1,0:T(8,128)(2,1)S(1)} %collective-permute-done.other_ref.other_fibres_ref), custom_call_target="tpu_custom_call" | custom-call | tf_op jit(solution)/shard_map/pallas_call | solution.py:220
  100.0 17.1 %all_to_all.29 = f32[64,1,128]{2,1,0:T(1,128)S(1)} all-to-all(f32[64,1,128]{2,1,0:T(1,128)S(1)} %bitcast.17), channel_id=1, replica_groups=mesh['y'=4,'pair'=8,'side'=2,'core'=2,'run'=4] {'y','pair','side'}, dimensions={0} | all-to-all | bytes 65536 | tf_op jit(solution)/shard_map/all_to_all | solution.py:184
  117.1 0.9 shard_map.50
  (4 shorter events, 0.1 us)
Async XLA Ops:
  34.2 6.2 %collective-permute-start = (bf16[2,256,128]{2,1,0:T(8,128)(2,1)S(1)}, bf16[2,256,128]{2,1,0:T(8,128)(2,1)S(1)}, u32[]{:S(2)}, u32[]{:S(2)}) collective-permute-start(bf16[2,256,128]{2,1,0:T(8,128)(2,1)S(1)} %bitcast.13), channel_id=1, source_target_pairs={{0,4},{4,0},{1,5},{5,1},{2,6},{6,2},{3,7},{7,3},{8,12},{12,8},{9,1... | collective-permute-start | bytes 393224 | tf_op jit(solution)/shard_map/ppermute | solution.py:188
  71.9 18.6 %copy-start = (f32[512,64]{0,1:T(8,128)S(1)}, f32[512,64]{0,1:T(8,128)}, u32[]{:S(2)}) copy-start(f32[512,64]{0,1:T(8,128)} %param.7) | copy-start | bytes 393220
  84.0 7.7 %collective-permute-start.1 = (f32[640,128]{1,0:T(8,128)S(1)}, f32[640,128]{1,0:T(8,128)S(1)}, u32[]{:S(2)}, u32[]{:S(2)}) collective-permute-start(f32[640,128]{1,0:T(8,128)S(1)} %bitcast.10), channel_id=1, source_target_pairs={{0,4},{4,0},{1,5},{5,1},{2,6},{6,2},{3,7},{7,3},{8,12},{12,8},{9,1... | collective-permute-start | bytes 983048 | tf_op jit(solution)/shard_map/ppermute | solution.py:188

commit v6 on v5

--- a/solution.py
+++ b/solution.py
@@ -8,6 +8,8 @@
 K = 64
 ITERS = 3
 LANES = 128
+WINDOW = 10
+CHUNKS = 4
 HIGHEST = lax.Precision.HIGHEST
 VMEM = pl.BlockSpec(memory_space=pltpu.VMEM)
 HBM = pl.BlockSpec(memory_space=pltpu.HBM)
@@ -46,14 +48,22 @@
 
 
 def weigh_kernel(slab_hbm, chord_hbm, span_hbm, out_ref, slab_ref, chord_ref, span_ref, sems):
-    copies = [
-        pltpu.make_async_copy(slab_hbm, slab_ref, sems.at[0]),
-        pltpu.make_async_copy(chord_hbm, chord_ref, sems.at[1]),
-        pltpu.make_async_copy(span_hbm, span_ref, sems.at[2]),
+    weights = [
+        pltpu.make_async_copy(chord_hbm, chord_ref, sems.at[0]),
+        pltpu.make_async_copy(span_hbm, span_ref, sems.at[1]),
     ]
-    for copy in copies:
+    width = slab_ref.shape[2] // CHUNKS
+    chunks = []
+    for at in range(CHUNKS):
+        part = pl.ds(at * width, width)
+        chunks.append(
+            pltpu.make_async_copy(
+                slab_hbm.at[:, :, part], slab_ref.at[:, :, part], sems.at[2 + at]
+            )
+        )
+    for copy in weights + chunks:
         copy.start()
-    for copy in copies[::-1]:
+    for copy in weights:
         copy.wait()
     lane = lax.broadcasted_iota(jnp.int32, (1, LANES), 1)
     row = lax.broadcasted_iota(jnp.int32, (out_ref.shape[1], LANES), 0)
@@ -67,7 +77,10 @@
         return block * chord * stations
 
     low_half = lane % K < K // 2
-    for chip in range(out_ref.shape[0] // 2):
+    chips = out_ref.shape[0] // 2
+    for chip in range(chips):
+        if chip % (chips // CHUNKS) == 0:
+            chunks[chip // (chips // CHUNKS)].wait()
         first, second = weigh(2 * chip), weigh(2 * chip + 1)
         low = jnp.where(low_half, first, pltpu.roll(second, K // 2, 1))
         high = jnp.where(low_half, pltpu.roll(first, LANES - K // 2, 1), second)
@@ -99,30 +112,32 @@
     both = jnp.concatenate([small, eye.astype(jnp.float32)], axis=1)
     blocks = [both[8 * b : 8 * b + 8] for b in range(n // 8)]
     sub = lax.broadcasted_iota(jnp.int32, wide, 0)
-    rows = []
-    for own in range(n // 8):
-        panel = [
-            {
-                b: jnp.broadcast_to(blocks[b][:, 8 * own + k : 8 * own + k + 1], wide)
-                for b in range(own, n // 8)
-            }
-            for k in range(8)
-        ]
-        pivots = None
-        for k in range(8):
-            pivot = jnp.broadcast_to(panel[k][own][k : k + 1], wide)
-            pivots = pivot if pivots is None else jnp.where(sub >= k, pivot, pivots)
-            inverse = 1.0 / pivot
-            row = jnp.broadcast_to(blocks[own][k : k + 1], wide) * inverse
-            column = dict(panel[k])
-            column[own] = jnp.where(sub > k, column[own], 0.0)
-            for later in range(k + 1, 8):
-                scale = jnp.broadcast_to(panel[later][own][k : k + 1], wide) * inverse
-                for b in range(own, n // 8):
-                    panel[later][b] = panel[later][b] - column[b] * scale
+
+    def spread(column, since):
+        return {
+            b: jnp.broadcast_to(blocks[b][:, column : column + 1], wide)
+            for b in range(since, n // 8)
+        }
+
+    ahead = {column: spread(column, 0) for column in range(WINDOW)}
+    pivots = [None] * (n // 8)
+    for j in range(n):
+        own, k = divmod(j, 8)
+        column = ahead.pop(j)
+        pivot = jnp.broadcast_to(column[own][k : k + 1], wide)
+        pivots[own] = pivot if k == 0 else jnp.where(sub >= k, pivot, pivots[own])
+        inverse = 1.0 / pivot
+        row = jnp.broadcast_to(blocks[own][k : k + 1], wide) * inverse
+        column[own] = jnp.where(sub > k, column[own], 0.0)
+        for later in ahead.values():
+            scale = jnp.broadcast_to(later[own][k : k + 1], wide) * inverse
             for b in range(own, n // 8):
-                blocks[b] = blocks[b] - column[b] * row
-        rows.append(blocks[own][:, n:] * lax.rsqrt(pivots)[:, n:])
+                later[b] = later[b] - column[b] * scale
+        for b in range(own, n // 8):
+            blocks[b] = blocks[b] - column[b] * row
+        if j + WINDOW < n:
+            ahead[j + WINDOW] = spread(j + WINDOW, (j + 1) // 8)
+    rows = [block[:, n:] * lax.rsqrt(p)[:, n:] for block, p in zip(blocks, pivots)]
     return jnp.concatenate(rows, axis=0)
 
 
@@ -204,7 +219,7 @@
         pltpu.VMEM(slab.shape, slab.dtype),
         pltpu.SMEM(chord_weight.shape, jnp.float32),
         pltpu.SMEM(span_weight.shape, jnp.float32),
-        pltpu.SemaphoreType.DMA((3,)),
+        pltpu.SemaphoreType.DMA((2 + CHUNKS,)),
     ]
     send = call(weigh_kernel, (tiles, rows, LANES), jnp.bfloat16, [HBM] * 3, scratch)(
         *(pltpu.with_memory_space_constraint(array, pltpu.HBM) for array in inputs)

time: 118 us -> 118 us (level)
  no operation moved by 1% of the time
where the time goes in v6:
time: 118 us; the launch traced here: 117 us
  blocking collectives  93.2 us (79%)
  starting transfers between devices  11.7 us (10%)
  Pallas kernels  10.2 us (9%)
  waiting for transfers between devices  1.77 us (2%)
    all_to_all x5, blocking collectives, swap(): return lax.all_to_all(array, axes, 0, 0, tiled=True)  93.2 us
    ppermute x2, starting transfers between devices, to_other_core(): return lax.ppermute(array, 'core', [(0, 1), (1, 0)])  11.7 us
    pallas_call x1, Pallas kernels, per_device(): call(factor_kernel, (rank, LANES), jnp.float32, [VMEM] * 5, [pltpu.VMEM((...  7.39 us
  transfers between devices with their start and end apart: 2, of which 2 were waited for; matrix products, arithmetic and copies ran while one was open for 0% of the time, Pallas kernels for 0%

profile of v6, /device:TPU:1, one launch (start us, length us, event | category | flops | bytes accessed | tf_op | source)
XLA Modules:
  0.0 117.2 jit_solution(12824097312052897188)
XLA Ops:
  0.0 1.2 %shard_map.46 = bf16[128,4,128]{2,1,0:T(4,128)(2,1)S(1)} custom-call(bf16[1,4,16384]{2,1,0:T(4,128)(2,1)} %slab_hbm.1, f32[4]{0:T(128)} %chord_hbm.1, f32[256]{0:T(256)} %span_hbm.1), custom_call_target="tpu_custom_call" | custom-call | tf_op jit(solution)/shard_map/pallas_call | solution.py:224
  1.2 33.0 %all_to_all.25 = bf16[64,2,4,128]{3,2,1,0:T(4,128)(2,1)S(1)} all-to-all(bf16[64,2,4,128]{3,2,1,0:T(4,128)(2,1)S(1)} %bitcast.16), channel_id=1, replica_groups=mesh['y'=4,'pair'=8,'side'=2,'core'=2,'run'=4] {'y','pair','side'}, dimensions={0} | all-to-all | bytes 262144 | tf_op jit(solution)/shard_map/all_to_all | solution.py:199
  34.3 5.2 %collective-permute-start = (bf16[2,256,128]{2,1,0:T(8,128)(2,1)S(1)}, bf16[2,256,128]{2,1,0:T(8,128)(2,1)S(1)}, u32[]{:S(2)}, u32[]{:S(2)}) collective-permute-start(bf16[2,256,128]{2,1,0:T(8,128)(2,1)S(1)} %bitcast.13), channel_id=1, source_target_pairs={{0,4},{4,0},{1,5},{5,1},{2,6},{6,2},{3,7},{7,3},{8,12},{12,8},{9,1... | collective-permute-start | bytes 393224 | tf_op jit(solution)/shard_map/ppermute | solution.py:203
  39.6 1.0 collective-permute-done.other_ref.other_fibres_ref
  40.6 0.3 shard_map.47
  40.9 15.8 %all_to_all.26 = f32[32,5,4,128]{3,2,1,0:T(4,128)S(1)} all-to-all(f32[32,5,4,128]{3,2,1,0:T(4,128)S(1)} %bitcast.12), channel_id=1, replica_groups=mesh['y'=4,'pair'=8,'side'=2,'core'=2,'run'=4] {'y','run','side'}, dimensions={0} | all-to-all | bytes 655360 | tf_op jit(solution)/shard_map/all_to_all | solution.py:199
  56.7 0.1 reduce_sum.18
  56.8 15.1 %all_to_all.27 = f32[8,5,4,128]{3,2,1,0:T(4,128)S(1)} all-to-all(f32[8,5,4,128]{3,2,1,0:T(4,128)S(1)} %broadcast_in_dim.4), channel_id=1, replica_groups=mesh['y'=4,'pair'=8,'side'=2,'core'=2,'run'=4] {'pair'}, dimensions={0} | all-to-all | bytes 163840 | tf_op jit(solution)/shard_map/all_to_all | solution.py:199
  72.0 0.0 copy-start
  72.0 12.1 %all_to_all.28 = f32[32,5,4,128]{3,2,1,0:T(4,128)S(1)} all-to-all(f32[32,5,4,128]{3,2,1,0:T(4,128)S(1)} %broadcast_in_dim.5), channel_id=1, replica_groups=mesh['y'=4,'pair'=8,'side'=2,'core'=2,'run'=4] {'y','run','side'}, dimensions={0} | all-to-all | bytes 655360 | tf_op jit(solution)/shard_map/all_to_all | solution.py:199
  84.1 6.5 %collective-permute-start.1 = (f32[640,128]{1,0:T(8,128)S(1)}, f32[640,128]{1,0:T(8,128)S(1)}, u32[]{:S(2)}, u32[]{:S(2)}) collective-permute-start(f32[640,128]{1,0:T(8,128)S(1)} %bitcast.10), channel_id=1, source_target_pairs={{0,4},{4,0},{1,5},{5,1},{2,6},{6,2},{3,7},{7,3},{8,12},{12,8},{9,1... | collective-permute-start | bytes 983048 | tf_op jit(solution)/shard_map/ppermute | solution.py:203
  90.6 0.0 copy-done
  90.6 0.4 shard_map.48.start_ref
  91.0 0.8 collective-permute-done.1.other_ref
  91.8 7.4 %shard_map.49 = f32[64,128]{1,0:T(8,128)S(1)} custom-call(f32[640,128]{1,0:T(8,128)S(1)} %bitcast.11, f32[640,128]{1,0:T(8,128)S(1)} %collective-permute-done.1.other_ref, f32[64,512]{1,0:T(8,128)S(1)} %shard_map.48.start_ref, bf16[2,256,128]{2,1,0:T(8,128)(2,1)S(1)} %bitcast.15, bf16[2,256,128]{2,1,0:T(8,128)(2,1)S(1)} %collective-permute-done.other_ref.other_fibres_ref), custom_call_target="tpu_custom_call" | custom-call | tf_op jit(solution)/shard_map/pallas_call | solution.py:235
  99.2 17.1 %all_to_all.29 = f32[64,1,128]{2,1,0:T(1,128)S(1)} all-to-all(f32[64,1,128]{2,1,0:T(1,128)S(1)} %bitcast.17), channel_id=1, replica_groups=mesh['y'=4,'pair'=8,'side'=2,'core'=2,'run'=4] {'y','pair','side'}, dimensions={0} | all-to-all | bytes 65536 | tf_op jit(solution)/shard_map/all_to_all | solution.py:199
  116.3 0.9 shard_map.50
  (4 shorter events, 0.1 us)
Async XLA Ops:
  34.3 6.2 %collective-permute-start = (bf16[2,256,128]{2,1,0:T(8,128)(2,1)S(1)}, bf16[2,256,128]{2,1,0:T(8,128)(2,1)S(1)}, u32[]{:S(2)}, u32[]{:S(2)}) collective-permute-start(bf16[2,256,128]{2,1,0:T(8,128)(2,1)S(1)} %bitcast.13), channel_id=1, source_target_pairs={{0,4},{4,0},{1,5},{5,1},{2,6},{6,2},{3,7},{7,3},{8,12},{12,8},{9,1... | collective-permute-start | bytes 393224 | tf_op jit(solution)/shard_map/ppermute | solution.py:203
  72.0 18.6 %copy-start = (f32[512,64]{0,1:T(8,128)S(1)}, f32[512,64]{0,1:T(8,128)}, u32[]{:S(2)}) copy-start(f32[512,64]{0,1:T(8,128)} %param.7) | copy-start | bytes 393220
  84.1 7.7 %collective-permute-start.1 = (f32[640,128]{1,0:T(8,128)S(1)}, f32[640,128]{1,0:T(8,128)S(1)}, u32[]{:S(2)}, u32[]{:S(2)}) collective-permute-start(f32[640,128]{1,0:T(8,128)S(1)} %bitcast.10), channel_id=1, source_target_pairs={{0,4},{4,0},{1,5},{5,1},{2,6},{6,2},{3,7},{7,3},{8,12},{12,8},{9,1... | collective-permute-start | bytes 983048 | tf_op jit(solution)/shard_map/ppermute | solution.py:203

commit v7 on v6

--- a/solution.py
+++ b/solution.py
@@ -9,7 +9,6 @@
 ITERS = 3
 LANES = 128
 WINDOW = 10
-CHUNKS = 4
 HIGHEST = lax.Precision.HIGHEST
 VMEM = pl.BlockSpec(memory_space=pltpu.VMEM)
 HBM = pl.BlockSpec(memory_space=pltpu.HBM)
@@ -48,22 +47,14 @@
 
 
 def weigh_kernel(slab_hbm, chord_hbm, span_hbm, out_ref, slab_ref, chord_ref, span_ref, sems):
-    weights = [
-        pltpu.make_async_copy(chord_hbm, chord_ref, sems.at[0]),
-        pltpu.make_async_copy(span_hbm, span_ref, sems.at[1]),
+    copies = [
+        pltpu.make_async_copy(slab_hbm, slab_ref, sems.at[0]),
+        pltpu.make_async_copy(chord_hbm, chord_ref, sems.at[1]),
+        pltpu.make_async_copy(span_hbm, span_ref, sems.at[2]),
     ]
-    width = slab_ref.shape[2] // CHUNKS
-    chunks = []
-    for at in range(CHUNKS):
-        part = pl.ds(at * width, width)
-        chunks.append(
-            pltpu.make_async_copy(
-                slab_hbm.at[:, :, part], slab_ref.at[:, :, part], sems.at[2 + at]
-            )
-        )
-    for copy in weights + chunks:
+    for copy in copies:
         copy.start()
-    for copy in weights:
+    for copy in copies[::-1]:
         copy.wait()
     lane = lax.broadcasted_iota(jnp.int32, (1, LANES), 1)
     row = lax.broadcasted_iota(jnp.int32, (out_ref.shape[1], LANES), 0)
@@ -77,10 +68,7 @@
         return block * chord * stations
 
     low_half = lane % K < K // 2
-    chips = out_ref.shape[0] // 2
-    for chip in range(chips):
-        if chip % (chips // CHUNKS) == 0:
-            chunks[chip // (chips // CHUNKS)].wait()
+    for chip in range(out_ref.shape[0] // 2):
         first, second = weigh(2 * chip), weigh(2 * chip + 1)
         low = jnp.where(low_half, first, pltpu.roll(second, K // 2, 1))
         high = jnp.where(low_half, pltpu.roll(first, LANES - K // 2, 1), second)
@@ -157,12 +145,10 @@
     out_ref[...] = start
 
 
-def factor_kernel(own_ref, other_ref, start_ref, own_fibres_ref, other_fibres_ref, out_ref, gram_ref):
+def factor_kernel(packed_ref, start_ref, own_fibres_ref, other_fibres_ref, out_ref, gram_ref):
     core = lax.axis_index("core")
     for at, (i, j) in enumerate(PAIRS):
-        rows = pl.ds(at % 5 * 128, 128)
-        mine = core == at // 5
-        block = jnp.where(mine, own_ref[rows, :], other_ref[rows, :])
+        block = packed_ref[at * 128 : (at + 1) * 128, :]
         gram_ref[i * 128 : (i + 1) * 128, j * 128 : (j + 1) * 128] = block
         if i != j:
             gram_ref[j * 128 : (j + 1) * 128, i * 128 : (i + 1) * 128] = block.T
@@ -203,12 +189,13 @@
     return lax.ppermute(array, "core", [(0, 1), (1, 0)])
 
 
-def sum_everywhere(packed):
+def sum_everywhere(half):
     shards = 32
-    shard = (packed.shape[0] // shards // 4, 4, LANES)
-    part = swap(packed.reshape(shards, *shard), PLANE).sum(0)
+    shard = (half.shape[0] // shards // 4, 4, LANES)
+    part = swap(half.reshape(shards, *shard), PLANE).sum(0)
     part = swap(jnp.broadcast_to(part[None], (8, *shard)), "pair").sum(0)
-    return swap(jnp.broadcast_to(part[None], (shards, *shard)), PLANE).reshape(packed.shape)
+    part = jnp.broadcast_to(part[None], (2 * shards, *shard))
+    return swap(part, ("core", *PLANE)).reshape(2 * half.shape[0], LANES)
 
 
 def per_device(slab, chord_weight, span_weight, start):
@@ -219,7 +206,7 @@
         pltpu.VMEM(slab.shape, slab.dtype),
         pltpu.SMEM(chord_weight.shape, jnp.float32),
         pltpu.SMEM(span_weight.shape, jnp.float32),
-        pltpu.SemaphoreType.DMA((2 + CHUNKS,)),
+        pltpu.SemaphoreType.DMA((3,)),
     ]
     send = call(weigh_kernel, (tiles, rows, LANES), jnp.bfloat16, [HBM] * 3, scratch)(
         *(pltpu.with_memory_space_constraint(array, pltpu.HBM) for array in inputs)
@@ -231,14 +218,14 @@
     chords, rank = start.shape
     ordered = call(order_kernel, (rank, chords), jnp.float32, [VMEM])(start.T)
     half = call(gram_kernel, (len(PAIRS) // 2 * 128, 128), jnp.float32, [VMEM] * 2)(own, other)
-    half = sum_everywhere(half)
+    packed = sum_everywhere(half)
     parts = call(
         factor_kernel,
         (rank, LANES),
         jnp.float32,
-        [VMEM] * 5,
+        [VMEM] * 4,
         [pltpu.VMEM((chords, chords), jnp.float32)],
-    )(half, to_other_core(half), ordered, own, other)
+    )(packed, ordered, own, other)
     parts = swap(parts.reshape(rank, 1, LANES), CHIPS).reshape(rank, LANES)
     return call(unfold_kernel, (1, K // 2, 4 * rank), jnp.bfloat16, [VMEM])(parts)
 

time: 118 us -> 120 us (1.017)
  waiting for transfers between devices: 1.77 us -> 13.7 us
  blocking collectives: 93.2 us -> 81.7 us
    all_to_all x0 -> x1, waiting for transfers between devices: none -> 12.8 us  [swap(): return lax.all_to_all(array, axes, 0, 0, tiled=True)]
    all_to_all x5 -> x4, blocking collectives: 93.2 us -> 81.7 us  [swap(): return lax.all_to_all(array, axes, 0, 0, tiled=True)]
    all_to_all x0 -> x1, starting transfers between devices: none -> 7.33 us  [swap(): return lax.all_to_all(array, axes, 0, 0, tiled=True)]
    ppermute x2 -> x1, starting transfers between devices: 11.7 us -> 5.25 us  [to_other_core(): return lax.ppermute(array, 'core', [(0, 1), (1, 0)])]
where the time goes in v7:
time: 120 us; the launch traced here: 119 us
  blocking collectives  81.7 us (68%)
  waiting for transfers between devices  13.7 us (11%)
  starting transfers between devices  12.6 us (10%)
  Pallas kernels  10.1 us (8%)
    all_to_all x4, blocking collectives, swap(): return lax.all_to_all(array, axes, 0, 0, tiled=True)  81.7 us
    all_to_all x1, waiting for transfers between devices, swap(): return lax.all_to_all(array, axes, 0, 0, tiled=True)  12.8 us
    pallas_call x1, Pallas kernels, per_device(): call(factor_kernel, (rank, LANES), jnp.float32, [VMEM] * 4, [pltpu.VMEM((...  7.38 us
    all_to_all x1, starting transfers between devices, swap(): return lax.all_to_all(array, axes, 0, 0, tiled=True)  7.33 us
    ppermute x1, starting transfers between devices, to_other_core(): return lax.ppermute(array, 'core', [(0, 1), (1, 0)])  5.25 us
  transfers between devices with their start and end apart: 2, of which 2 were waited for; matrix products, arithmetic and copies ran while one was open for 0% of the time, Pallas kernels for 0%

profile of v7, /device:TPU:1, one launch (start us, length us, event | category | flops | bytes accessed | tf_op | source)
XLA Modules:
  0.0 119.3 jit_solution(11120054801474938302)
XLA Ops:
  0.0 1.1 shard_map.46
  1.1 33.0 %all_to_all.25 = bf16[64,2,4,128]{3,2,1,0:T(4,128)(2,1)S(1)} all-to-all(bf16[64,2,4,128]{3,2,1,0:T(4,128)(2,1)S(1)} %bitcast.15), channel_id=1, replica_groups=mesh['y'=4,'pair'=8,'side'=2,'core'=2,'run'=4] {'y','pair','side'}, dimensions={0} | all-to-all | bytes 262144 | tf_op jit(solution)/shard_map/all_to_all | solution.py:185
  34.2 5.2 %collective-permute-start = (bf16[2,256,128]{2,1,0:T(8,128)(2,1)S(1)}, bf16[2,256,128]{2,1,0:T(8,128)(2,1)S(1)}, u32[]{:S(2)}, u32[]{:S(2)}) collective-permute-start(bf16[2,256,128]{2,1,0:T(8,128)(2,1)S(1)} %bitcast.12), channel_id=1, source_target_pairs={{0,4},{4,0},{1,5},{5,1},{2,6},{6,2},{3,7},{7,3},{8,12},{12,8},{9,1... | collective-permute-start | bytes 393224 | tf_op jit(solution)/shard_map/ppermute | solution.py:189
  39.5 1.0 collective-permute-done.other_ref.other_fibres_ref
  40.4 0.3 shard_map.47
  40.8 15.8 %all_to_all.26 = f32[32,5,4,128]{3,2,1,0:T(4,128)S(1)} all-to-all(f32[32,5,4,128]{3,2,1,0:T(4,128)S(1)} %bitcast.11), channel_id=1, replica_groups=mesh['y'=4,'pair'=8,'side'=2,'core'=2,'run'=4] {'y','run','side'}, dimensions={0} | all-to-all | bytes 655360 | tf_op jit(solution)/shard_map/all_to_all | solution.py:185
  56.6 0.1 reduce_sum.18
  56.7 15.1 %all_to_all.27 = f32[8,5,4,128]{3,2,1,0:T(4,128)S(1)} all-to-all(f32[8,5,4,128]{3,2,1,0:T(4,128)S(1)} %broadcast_in_dim.4), channel_id=1, replica_groups=mesh['y'=4,'pair'=8,'side'=2,'core'=2,'run'=4] {'pair'}, dimensions={0} | all-to-all | bytes 163840 | tf_op jit(solution)/shard_map/all_to_all | solution.py:185
  71.9 0.9 broadcast_in_dim.5
  72.8 0.0 copy-start
  72.8 7.3 %all-to-all-start.3 = ((f32[64,5,4,128]{3,2,1,0:T(4,128)}), f32[64,5,4,128]{3,2,1,0:T(4,128)S(1)}, u32[]{:S(2)}, u32[]{:S(2)}) async-start(f32[64,5,4,128]{3,2,1,0:T(4,128)} %broadcast_in_dim.5), calls=%async_computation.3 | async-start | bytes 1310720 | tf_op jit(solution)/shard_map/all_to_all | solution.py:185
  80.1 0.0 copy-done
  80.1 0.4 shard_map.48.start_ref
  80.6 12.8 %all-to-all-done.3 = f32[64,5,4,128]{3,2,1,0:T(4,128)S(1)} async-done(((f32[64,5,4,128]{3,2,1,0:T(4,128)}), f32[64,5,4,128]{3,2,1,0:T(4,128)S(1)}, u32[]{:S(2)}, u32[]{:S(2)}) %all-to-all-start.3) | async-done | bytes 655392 | tf_op jit(solution)/shard_map/all_to_all | solution.py:185
  93.3 7.4 %shard_map.49 = f32[64,128]{1,0:T(8,128)S(1)} custom-call(f32[1280,128]{1,0:T(8,128)S(1)} %bitcast.10, f32[64,512]{1,0:T(8,128)S(1)} %shard_map.48.start_ref, bf16[2,256,128]{2,1,0:T(8,128)(2,1)S(1)} %bitcast.14, bf16[2,256,128]{2,1,0:T(8,128)(2,1)S(1)} %collective-permute-done.other_ref.other_fibres_ref), custom_call_target="tpu_custom_call" | custom-call | tf_op jit(solution)/shard_map/pallas_call | solution.py:222
  100.7 17.7 %all_to_all.28 = f32[64,1,128]{2,1,0:T(1,128)S(1)} all-to-all(f32[64,1,128]{2,1,0:T(1,128)S(1)} %bitcast.16), channel_id=1, replica_groups=mesh['y'=4,'pair'=8,'side'=2,'core'=2,'run'=4] {'y','pair','side'}, dimensions={0} | all-to-all | bytes 65536 | tf_op jit(solution)/shard_map/all_to_all | solution.py:185
  118.4 0.9 shard_map.50
  (3 shorter events, 0.1 us)
Async XLA Ops:
  34.2 6.2 %collective-permute-start = (bf16[2,256,128]{2,1,0:T(8,128)(2,1)S(1)}, bf16[2,256,128]{2,1,0:T(8,128)(2,1)S(1)}, u32[]{:S(2)}, u32[]{:S(2)}) collective-permute-start(bf16[2,256,128]{2,1,0:T(8,128)(2,1)S(1)} %bitcast.12), channel_id=1, source_target_pairs={{0,4},{4,0},{1,5},{5,1},{2,6},{6,2},{3,7},{7,3},{8,12},{12,8},{9,1... | collective-permute-start | bytes 393224 | tf_op jit(solution)/shard_map/ppermute | solution.py:189
  72.8 7.3 %copy-start = (f32[512,64]{0,1:T(8,128)S(1)}, f32[512,64]{0,1:T(8,128)}, u32[]{:S(2)}) copy-start(f32[512,64]{0,1:T(8,128)} %param.7) | copy-start | bytes 393220
  72.8 20.5 %all-to-all-start.3 = ((f32[64,5,4,128]{3,2,1,0:T(4,128)}), f32[64,5,4,128]{3,2,1,0:T(4,128)S(1)}, u32[]{:S(2)}, u32[]{:S(2)}) async-start(f32[64,5,4,128]{3,2,1,0:T(4,128)} %broadcast_in_dim.5), calls=%async_computation.3 | async-start | bytes 1310720 | tf_op jit(solution)/shard_map/all_to_all | solution.py:185

commit v8 on v7

--- a/solution.py
+++ b/solution.py
@@ -14,7 +14,7 @@
 HBM = pl.BlockSpec(memory_space=pltpu.HBM)
 CHIPS = ("y", "pair", "side")
 PLANE = ("y", "run", "side")
-PAIRS = [(0, 0), (0, 1), (1, 1), (0, 2), (1, 3), (2, 2), (2, 3), (3, 3), (2, 1), (3, 0)]
+PAIRS = [(i, j) for i in range(4) for j in range(i, 4)]
 
 
 def call(kernel, shape, dtype, specs, scratch=()):
@@ -76,21 +76,24 @@
         out_ref[2 * chip + 1] = high.astype(jnp.bfloat16)
 
 
-def gram_kernel(own_ref, other_ref, out_ref):
-    first = lax.axis_index("core") == 0
-    crossed = [(0, 2), (1, 3)]
-    for at, (i, j) in enumerate([(0, 0), (0, 1), (1, 1), *crossed]):
-        total = None
-        for part in range(2):
-            left = own_ref[part, i * 128 : (i + 1) * 128, :]
-            if j < 2:
-                right = own_ref[part, j * 128 : (j + 1) * 128, :]
-            else:
-                low, high = other_ref[part, :128, :], other_ref[part, 128:, :]
-                right = jnp.where(first == (j == 2), low, high)
-            term = nt(left, right)
-            total = term if total is None else total + term
-        out_ref[at * 128 : (at + 1) * 128, :] = total
+def gram_kernel(fibres_ref, out_ref):
+    core = lax.axis_index("core")
+    count = len(PAIRS) // 2
+
+    def make(pairs):
+        for at, (i, j) in enumerate(pairs):
+            left, right = pl.ds(i * 128, 128), pl.ds(j * 128, 128)
+            out_ref[at * 128 : (at + 1) * 128, :] = nt(
+                fibres_ref[0, left, :], fibres_ref[0, right, :]
+            ) + nt(fibres_ref[1, left, :], fibres_ref[1, right, :])
+
+    @pl.when(core == 0)
+    def _():
+        make(PAIRS[:count])
+
+    @pl.when(core != 0)
+    def _():
+        make(PAIRS[count:])
 
 
 def inverse_cholesky(small):
@@ -129,24 +132,7 @@
     return jnp.concatenate(rows, axis=0)
 
 
-def order_kernel(start_ref, out_ref):
-    chords = start_ref.shape[1]
-    source = lax.broadcasted_iota(jnp.int32, (chords, chords), 0)
-    target = lax.broadcasted_iota(jnp.int32, (chords, chords), 1)
-    half = chords // 2
-    wanted = target % half // 4 * 8 + target // half * 4 + target % 4
-    order = (source == wanted).astype(jnp.bfloat16)
-    rest = start_ref[...]
-    start = jnp.zeros_like(rest)
-    for _ in range(3):
-        part = rest.astype(jnp.bfloat16)
-        rest = rest - part.astype(jnp.float32)
-        start = start + nn(part, order)
-    out_ref[...] = start
-
-
-def factor_kernel(packed_ref, start_ref, own_fibres_ref, other_fibres_ref, out_ref, gram_ref):
-    core = lax.axis_index("core")
+def factor_kernel(packed_ref, start_ref, fibres_ref, out_ref, gram_ref):
     for at, (i, j) in enumerate(PAIRS):
         block = packed_ref[at * 128 : (at + 1) * 128, :]
         gram_ref[i * 128 : (i + 1) * 128, j * 128 : (j + 1) * 128] = block
@@ -158,12 +144,9 @@
         if iteration < ITERS - 1:
             product = nn(product, gram_ref[...], HIGHEST)
         product = nn(inverse_cholesky(small), product, HIGHEST)
-    half = gram_ref.shape[0] // 2
-    narrow = product.astype(jnp.bfloat16)
-    own = jnp.where(core == 0, own_fibres_ref[0], own_fibres_ref[1])
-    other = jnp.where(core == 0, other_fibres_ref[0], other_fibres_ref[1])
-    low, high = jnp.where(core == 0, own, other), jnp.where(core == 0, other, own)
-    ranked = nn(narrow[:, :half], low) + nn(narrow[:, half:], high)
+    core = lax.axis_index("core")
+    fibres = jnp.where(core == 0, fibres_ref[0], fibres_ref[1])
+    ranked = nn(product.astype(jnp.bfloat16), fibres)
     out_ref[...] = ranked.astype(jnp.bfloat16).astype(jnp.float32)
 
 
@@ -185,17 +168,16 @@
     return lax.all_to_all(array, axes, 0, 0, tiled=True)
 
 
-def to_other_core(array):
-    return lax.ppermute(array, "core", [(0, 1), (1, 0)])
-
-
-def sum_everywhere(half):
+def from_both_cores(array):
+    return lax.all_gather(array, "core", axis=0)
+
+
+def sum_everywhere(packed):
     shards = 32
-    shard = (half.shape[0] // shards // 4, 4, LANES)
-    part = swap(half.reshape(shards, *shard), PLANE).sum(0)
+    shard = (packed.shape[0] // shards // 4, 4, LANES)
+    part = swap(packed.reshape(shards, *shard), PLANE).sum(0)
     part = swap(jnp.broadcast_to(part[None], (8, *shard)), "pair").sum(0)
-    part = jnp.broadcast_to(part[None], (2 * shards, *shard))
-    return swap(part, ("core", *PLANE)).reshape(2 * half.shape[0], LANES)
+    return swap(jnp.broadcast_to(part[None], (shards, *shard)), PLANE).reshape(packed.shape)
 
 
 def per_device(slab, chord_weight, span_weight, start):
@@ -213,19 +195,19 @@
     )
     chips = tiles // 2
     received = swap(send.reshape(chips, 2, rows, LANES), CHIPS)
-    own = received.transpose(1, 0, 2, 3).reshape(2, chips * rows, LANES)
-    other = to_other_core(own)
+    received = from_both_cores(received.reshape(tiles * rows, LANES))
+    fibres = lax.optimization_barrier(received).reshape(2, chips, 2, rows, LANES)
+    fibres = fibres.transpose(2, 1, 0, 3, 4).reshape(2, tiles * rows, LANES)
+    half = call(gram_kernel, (len(PAIRS) // 2 * 128, 128), jnp.float32, [VMEM])(fibres)
+    packed = from_both_cores(sum_everywhere(half)).reshape(len(PAIRS) * 128, 128)
     chords, rank = start.shape
-    ordered = call(order_kernel, (rank, chords), jnp.float32, [VMEM])(start.T)
-    half = call(gram_kernel, (len(PAIRS) // 2 * 128, 128), jnp.float32, [VMEM] * 2)(own, other)
-    packed = sum_everywhere(half)
     parts = call(
         factor_kernel,
         (rank, LANES),
         jnp.float32,
-        [VMEM] * 4,
+        [VMEM] * 3,
         [pltpu.VMEM((chords, chords), jnp.float32)],
-    )(packed, ordered, own, other)
+    )(packed, start.T, fibres)
     parts = swap(parts.reshape(rank, 1, LANES), CHIPS).reshape(rank, LANES)
     return call(unfold_kernel, (1, K // 2, 4 * rank), jnp.bfloat16, [VMEM])(parts)
 

time: 120 us -> 115 us (0.958)
  blocking collectives: 81.7 us -> 105 us
  waiting for transfers between devices: 13.7 us -> 0 us
  starting transfers between devices: 12.6 us -> 0 us
    all_to_all x1 -> x0, waiting for transfers between devices: 12.8 us -> none  [swap(): return lax.all_to_all(array, axes, 0, 0, tiled=True)]
    all_gather x0 -> x2, blocking collectives: none -> 11.6 us  [from_both_cores(): return lax.all_gather(array, 'core', axis=0)]
    all_to_all x4 -> x5, blocking collectives: 81.7 us -> 93 us  [swap(): return lax.all_to_all(array, axes, 0, 0, tiled=True)]
    all_to_all x1 -> x0, starting transfers between devices: 7.33 us -> none  [swap(): return lax.all_to_all(array, axes, 0, 0, tiled=True)]
    ppermute x1 -> x0, starting transfers between devices: 5.25 us -> none  [to_other_core(): return lax.ppermute(array, 'core', [(0, 1), (1, 0)])]
    pallas_call x3 -> x2, Pallas kernels: 8.14 us -> 7.7 us  [the longest x1 7.34 us: per_device(): call(factor_kernel, (rank, LANES), jnp.float32, [VMEM] * 3, [pltpu.VMEM((...]
  transfers between devices with their start and end apart: 2 -> 0, of which waited for: 2 -> 0; matrix products, arithmetic and copies ran while one was open for 0% -> 0% of each run, Pallas kernels for 0% -> 0%
where the time goes in v8:
time: 115 us
  blocking collectives  105 us (91%)
  Pallas kernels  9.68 us (8%)
    all_to_all x5, blocking collectives, swap(): return lax.all_to_all(array, axes, 0, 0, tiled=True)  93 us
    all_gather x2, blocking collectives, from_both_cores(): return lax.all_gather(array, 'core', axis=0)  11.6 us
    pallas_call x1, Pallas kernels, per_device(): call(factor_kernel, (rank, LANES), jnp.float32, [VMEM] * 3, [pltpu.VMEM((...  7.34 us

profile of v8, /device:TPU:1, one launch (start us, length us, event | category | flops | bytes accessed | tf_op | source)
XLA Modules:
  0.0 114.5 jit_solution(16538719915547051296)
XLA Ops:
  0.0 1.1 shard_map.46
  1.1 33.0 %all_to_all.25 = bf16[64,2,4,128]{3,2,1,0:T(4,128)(2,1)S(1)} all-to-all(bf16[64,2,4,128]{3,2,1,0:T(4,128)(2,1)S(1)} %bitcast.18), channel_id=1, replica_groups=mesh['y'=4,'pair'=8,'side'=2,'core'=2,'run'=4] {'y','pair','side'}, dimensions={0} | all-to-all | bytes 262144 | tf_op jit(solution)/shard_map/all_to_all | solution.py:168
  34.2 5.0 %all_gather.6 = bf16[2,512,128]{2,1,0:T(8,128)(2,1)S(1)} all-gather(bf16[1,512,128]{2,1,0:T(8,128)(2,1)S(1)} %bitcast.24), channel_id=1, replica_groups=mesh['y'=4,'pair'=8,'side'=2,'core'=2,'run'=4] {'core'}, dimensions={0}, use_global_device_ids=true | all-gather | bytes 393216 | tf_op jit(solution)/shard_map/all_gather | solution.py:172
  39.1 0.1 copy.10
  39.2 0.4 shard_map.47
  39.6 15.8 %all_to_all.26 = f32[32,5,4,128]{3,2,1,0:T(4,128)S(1)} all-to-all(f32[32,5,4,128]{3,2,1,0:T(4,128)S(1)} %bitcast.17), channel_id=1, replica_groups=mesh['y'=4,'pair'=8,'side'=2,'core'=2,'run'=4] {'y','run','side'}, dimensions={0} | all-to-all | bytes 655360 | tf_op jit(solution)/shard_map/all_to_all | solution.py:168
  55.4 0.1 reduce_sum.18
  55.5 15.1 %all_to_all.27 = f32[8,5,4,128]{3,2,1,0:T(4,128)S(1)} all-to-all(f32[8,5,4,128]{3,2,1,0:T(4,128)S(1)} %broadcast_in_dim.4), channel_id=1, replica_groups=mesh['y'=4,'pair'=8,'side'=2,'core'=2,'run'=4] {'pair'}, dimensions={0} | all-to-all | bytes 163840 | tf_op jit(solution)/shard_map/all_to_all | solution.py:168
  70.7 11.9 %all_to_all.28 = f32[32,5,4,128]{3,2,1,0:T(4,128)S(1)} all-to-all(f32[32,5,4,128]{3,2,1,0:T(4,128)S(1)} %broadcast_in_dim.5), channel_id=1, replica_groups=mesh['y'=4,'pair'=8,'side'=2,'core'=2,'run'=4] {'y','run','side'}, dimensions={0} | all-to-all | bytes 655360 | tf_op jit(solution)/shard_map/all_to_all | solution.py:168
  82.6 0.0 copy-start
  82.6 6.6 %all_gather.7 = f32[2,640,128]{2,1,0:T(8,128)S(1)} all-gather(f32[1,640,128]{2,1,0:T(8,128)S(1)} %bitcast.22), channel_id=1, replica_groups=mesh['y'=4,'pair'=8,'side'=2,'core'=2,'run'=4] {'core'}, dimensions={0}, use_global_device_ids=true | all-gather | bytes 983040 | tf_op jit(solution)/shard_map/all_gather | solution.py:172
  89.2 0.0 copy-done
  89.2 7.3 %shard_map.48 = f32[64,128]{1,0:T(8,128)S(1)} custom-call(f32[1280,128]{1,0:T(8,128)S(1)} %bitcast.14, f32[64,512]{1,0:T(8,128)S(1)} %bitcast.19, bf16[2,512,128]{2,1,0:T(8,128)(2,1)S(1)} %bitcast.16), custom_call_target="tpu_custom_call" | custom-call | tf_op jit(solution)/shard_map/pallas_call | solution.py:204
  96.6 17.1 %all_to_all.29 = f32[64,1,128]{2,1,0:T(1,128)S(1)} all-to-all(f32[64,1,128]{2,1,0:T(1,128)S(1)} %bitcast.20), channel_id=1, replica_groups=mesh['y'=4,'pair'=8,'side'=2,'core'=2,'run'=4] {'y','pair','side'}, dimensions={0} | all-to-all | bytes 65536 | tf_op jit(solution)/shard_map/all_to_all | solution.py:168
  113.7 0.9 shard_map.49
  (3 shorter events, 0.1 us)
Async XLA Ops:
  82.6 6.6 %copy-start = (f32[512,64]{0,1:T(8,128)S(1)}, f32[512,64]{0,1:T(8,128)}, u32[]{:S(2)}) copy-start(f32[512,64]{0,1:T(8,128)} %param.7) | copy-start | bytes 393220

commit v9 on v8

--- a/solution.py
+++ b/solution.py
@@ -14,7 +14,8 @@
 HBM = pl.BlockSpec(memory_space=pltpu.HBM)
 CHIPS = ("y", "pair", "side")
 PLANE = ("y", "run", "side")
-PAIRS = [(i, j) for i in range(4) for j in range(i, 4)]
+SHARES = [((0, 1), [(0, 1), (0, 2), (0, 3)]), ((2, 3), [(1, 2), (1, 3), (2, 3)])]
+SHARE_ROWS = 576
 
 
 def call(kernel, shape, dtype, specs, scratch=()):
@@ -76,24 +77,31 @@
         out_ref[2 * chip + 1] = high.astype(jnp.bfloat16)
 
 
+def square_indices():
+    return (lax.broadcasted_iota(jnp.int32, (128, 128), axis) for axis in range(2))
+
+
 def gram_kernel(fibres_ref, out_ref):
     core = lax.axis_index("core")
-    count = len(PAIRS) // 2
-
-    def make(pairs):
-        for at, (i, j) in enumerate(pairs):
-            left, right = pl.ds(i * 128, 128), pl.ds(j * 128, 128)
-            out_ref[at * 128 : (at + 1) * 128, :] = nt(
-                fibres_ref[0, left, :], fibres_ref[0, right, :]
-            ) + nt(fibres_ref[1, left, :], fibres_ref[1, right, :])
-
-    @pl.when(core == 0)
-    def _():
-        make(PAIRS[:count])
-
-    @pl.when(core != 0)
-    def _():
-        make(PAIRS[count:])
+
+    def block(i, j):
+        left, right = pl.ds(i * 128, 128), pl.ds(j * 128, 128)
+        return nt(fibres_ref[0, left, :], fibres_ref[0, right, :]) + nt(
+            fibres_ref[1, left, :], fibres_ref[1, right, :]
+        )
+
+    def make(diagonal, pairs):
+        row, column = square_indices()
+        first, second = (block(i, i) for i in diagonal)
+        out_ref[:128, :] = jnp.where(row <= column, first, second)
+        for at, (i, j) in enumerate(pairs, 1):
+            out_ref[at * 128 : (at + 1) * 128, :] = block(i, j)
+        rest = jnp.sum(jnp.where(row == column, second, 0.0), axis=0, keepdims=True)
+        row = row[: SHARE_ROWS - 512]
+        out_ref[512:, :] = jnp.where(row == 0, rest, 0.0)
+
+    for own, share in enumerate(SHARES):
+        pl.when(core == own)(lambda share=share: make(*share))
 
 
 def inverse_cholesky(small):
@@ -133,11 +141,21 @@
 
 
 def factor_kernel(packed_ref, start_ref, fibres_ref, out_ref, gram_ref):
-    for at, (i, j) in enumerate(PAIRS):
-        block = packed_ref[at * 128 : (at + 1) * 128, :]
+    def put(i, j, block):
         gram_ref[i * 128 : (i + 1) * 128, j * 128 : (j + 1) * 128] = block
-        if i != j:
-            gram_ref[j * 128 : (j + 1) * 128, i * 128 : (i + 1) * 128] = block.T
+
+    row, column = square_indices()
+    for own, ((first, second), pairs) in enumerate(SHARES):
+        base = own * SHARE_ROWS
+        mixed = packed_ref[base : base + 128, :]
+        flipped, diagonal = mixed.T, packed_ref[base + 512 : base + 513, :]
+        put(first, first, jnp.where(row <= column, mixed, flipped))
+        other = jnp.where(row > column, mixed, flipped)
+        put(second, second, jnp.where(row == column, diagonal, other))
+        for at, (i, j) in enumerate(pairs, 1):
+            block = packed_ref[base + at * 128 : base + (at + 1) * 128, :]
+            put(i, j, block)
+            put(j, i, block.T)
     product = nn(start_ref[...], gram_ref[...], HIGHEST)
     for iteration in range(ITERS):
         small = nt(product, product, HIGHEST)
@@ -174,7 +192,7 @@
 
 def sum_everywhere(packed):
     shards = 32
-    shard = (packed.shape[0] // shards // 4, 4, LANES)
+    shard = (packed.shape[0] // shards // 2, 2, LANES)
     part = swap(packed.reshape(shards, *shard), PLANE).sum(0)
     part = swap(jnp.broadcast_to(part[None], (8, *shard)), "pair").sum(0)
     return swap(jnp.broadcast_to(part[None], (shards, *shard)), PLANE).reshape(packed.shape)
@@ -198,8 +216,8 @@
     received = from_both_cores(received.reshape(tiles * rows, LANES))
     fibres = lax.optimization_barrier(received).reshape(2, chips, 2, rows, LANES)
     fibres = fibres.transpose(2, 1, 0, 3, 4).reshape(2, tiles * rows, LANES)
-    half = call(gram_kernel, (len(PAIRS) // 2 * 128, 128), jnp.float32, [VMEM])(fibres)
-    packed = from_both_cores(sum_everywhere(half)).reshape(len(PAIRS) * 128, 128)
+    share = call(gram_kernel, (SHARE_ROWS, LANES), jnp.float32, [VMEM])(fibres)
+    packed = from_both_cores(sum_everywhere(share)).reshape(2 * SHARE_ROWS, LANES)
     chords, rank = start.shape
     parts = call(
         factor_kernel,

time: 115 us -> 114 us (level)
  no operation moved by 1% of the time
where the time goes in v9:
time: 114 us
  blocking collectives  104 us (91%)
  Pallas kernels  9.67 us (8%)
    all_to_all x5, blocking collectives, swap(): return lax.all_to_all(array, axes, 0, 0, tiled=True)  92.2 us
    all_gather x2, blocking collectives, from_both_cores(): return lax.all_gather(array, 'core', axis=0)  11.7 us
    pallas_call x1, Pallas kernels, per_device(): call(factor_kernel, (rank, LANES), jnp.float32, [VMEM] * 3, [pltpu.VMEM((...  7.33 us

profile of v9, /device:TPU:1, one launch (start us, length us, event | category | flops | bytes accessed | tf_op | source)
XLA Modules:
  0.0 113.9 jit_solution(7631330220699614121)
XLA Ops:
  0.0 1.1 shard_map.46
  1.1 33.0 %all_to_all.25 = bf16[64,2,4,128]{3,2,1,0:T(4,128)(2,1)S(1)} all-to-all(bf16[64,2,4,128]{3,2,1,0:T(4,128)(2,1)S(1)} %bitcast.18), channel_id=1, replica_groups=mesh['y'=4,'pair'=8,'side'=2,'core'=2,'run'=4] {'y','pair','side'}, dimensions={0} | all-to-all | bytes 262144 | tf_op jit(solution)/shard_map/all_to_all | solution.py:186
  34.2 5.0 %all_gather.6 = bf16[2,512,128]{2,1,0:T(8,128)(2,1)S(1)} all-gather(bf16[1,512,128]{2,1,0:T(8,128)(2,1)S(1)} %bitcast.24), channel_id=1, replica_groups=mesh['y'=4,'pair'=8,'side'=2,'core'=2,'run'=4] {'core'}, dimensions={0}, use_global_device_ids=true | all-gather | bytes 393216 | tf_op jit(solution)/shard_map/all_gather | solution.py:190
  39.1 0.1 copy.10
  39.2 0.4 shard_map.47
  39.6 15.5 %all_to_all.26 = f32[32,9,2,128]{3,2,1,0:T(2,128)S(1)} all-to-all(f32[32,9,2,128]{3,2,1,0:T(2,128)S(1)} %bitcast.17), channel_id=1, replica_groups=mesh['y'=4,'pair'=8,'side'=2,'core'=2,'run'=4] {'y','run','side'}, dimensions={0} | all-to-all | bytes 589824 | tf_op jit(solution)/shard_map/all_to_all | solution.py:186
  55.1 0.1 reduce_sum.18
  55.2 15.0 %all_to_all.27 = f32[8,9,2,128]{3,2,1,0:T(2,128)S(1)} all-to-all(f32[8,9,2,128]{3,2,1,0:T(2,128)S(1)} %broadcast_in_dim.4), channel_id=1, replica_groups=mesh['y'=4,'pair'=8,'side'=2,'core'=2,'run'=4] {'pair'}, dimensions={0} | all-to-all | bytes 147456 | tf_op jit(solution)/shard_map/all_to_all | solution.py:186
  70.3 0.1 broadcast_in_dim.5
  70.4 11.5 %all_to_all.28 = f32[32,9,2,128]{3,2,1,0:T(2,128)S(1)} all-to-all(f32[32,9,2,128]{3,2,1,0:T(2,128)S(1)} %broadcast_in_dim.5), channel_id=1, replica_groups=mesh['y'=4,'pair'=8,'side'=2,'core'=2,'run'=4] {'y','run','side'}, dimensions={0} | all-to-all | bytes 589824 | tf_op jit(solution)/shard_map/all_to_all | solution.py:186
  81.9 0.0 copy-start
  81.9 6.8 %all_gather.7 = f32[2,576,128]{2,1,0:T(8,128)S(1)} all-gather(f32[1,576,128]{2,1,0:T(8,128)S(1)} %bitcast.22), channel_id=1, replica_groups=mesh['y'=4,'pair'=8,'side'=2,'core'=2,'run'=4] {'core'}, dimensions={0}, use_global_device_ids=true | all-gather | bytes 884736 | tf_op jit(solution)/shard_map/all_gather | solution.py:190
  88.6 0.0 copy-done
  88.6 7.3 %shard_map.48 = f32[64,128]{1,0:T(8,128)S(1)} custom-call(f32[1152,128]{1,0:T(8,128)S(1)} %bitcast.14, f32[64,512]{1,0:T(8,128)S(1)} %bitcast.21, bf16[2,512,128]{2,1,0:T(8,128)(2,1)S(1)} %bitcast.16), custom_call_target="tpu_custom_call" | custom-call | tf_op jit(solution)/shard_map/pallas_call | solution.py:222
  96.0 17.1 %all_to_all.29 = f32[64,1,128]{2,1,0:T(1,128)S(1)} all-to-all(f32[64,1,128]{2,1,0:T(1,128)S(1)} %bitcast.19), channel_id=1, replica_groups=mesh['y'=4,'pair'=8,'side'=2,'core'=2,'run'=4] {'y','pair','side'}, dimensions={0} | all-to-all | bytes 65536 | tf_op jit(solution)/shard_map/all_to_all | solution.py:186
  113.0 0.9 shard_map.49
  (2 shorter events, 0.1 us)
Async XLA Ops:
  81.9 6.8 %copy-start = (f32[512,64]{0,1:T(8,128)S(1)}, f32[512,64]{0,1:T(8,128)}, u32[]{:S(2)}) copy-start(f32[512,64]{0,1:T(8,128)} %param.7) | copy-start | bytes 393220

commit v10 on v9

--- a/solution.py
+++ b/solution.py
@@ -15,7 +15,7 @@
 CHIPS = ("y", "pair", "side")
 PLANE = ("y", "run", "side")
 SHARES = [((0, 1), [(0, 1), (0, 2), (0, 3)]), ((2, 3), [(1, 2), (1, 3), (2, 3)])]
-SHARE_ROWS = 576
+SHARE_ROWS = 544
 
 
 def call(kernel, shape, dtype, specs, scratch=()):
@@ -192,7 +192,7 @@
 
 def sum_everywhere(packed):
     shards = 32
-    shard = (packed.shape[0] // shards // 2, 2, LANES)
+    shard = (packed.shape[0] // shards, 1, LANES)
     part = swap(packed.reshape(shards, *shard), PLANE).sum(0)
     part = swap(jnp.broadcast_to(part[None], (8, *shard)), "pair").sum(0)
     return swap(jnp.broadcast_to(part[None], (shards, *shard)), PLANE).reshape(packed.shape)

time: 114 us -> 114 us (level)
  no operation moved by 1% of the time
where the time goes in v10:
time: 114 us
  blocking collectives  104 us (91%)
  Pallas kernels  9.67 us (8%)
    all_to_all x5, blocking collectives, swap(): return lax.all_to_all(array, axes, 0, 0, tiled=True)  91.7 us
    all_gather x2, blocking collectives, from_both_cores(): return lax.all_gather(array, 'core', axis=0)  11.8 us
    pallas_call x1, Pallas kernels, per_device(): call(factor_kernel, (rank, LANES), jnp.float32, [VMEM] * 3, [pltpu.VMEM((...  7.33 us

profile of v10, /device:TPU:1, one launch (start us, length us, event | category | flops | bytes accessed | tf_op | source)
XLA Modules:
  0.0 113.7 jit_solution(6279134204583318124)
XLA Ops:
  0.0 1.1 shard_map.46
  1.1 33.0 %all_to_all.25 = bf16[64,2,4,128]{3,2,1,0:T(4,128)(2,1)S(1)} all-to-all(bf16[64,2,4,128]{3,2,1,0:T(4,128)(2,1)S(1)} %bitcast.20), channel_id=1, replica_groups=mesh['y'=4,'pair'=8,'side'=2,'core'=2,'run'=4] {'y','pair','side'}, dimensions={0} | all-to-all | bytes 262144 | tf_op jit(solution)/shard_map/all_to_all | solution.py:186
  34.2 5.0 %all_gather.6 = bf16[2,512,128]{2,1,0:T(8,128)(2,1)S(1)} all-gather(bf16[1,512,128]{2,1,0:T(8,128)(2,1)S(1)} %bitcast.26), channel_id=1, replica_groups=mesh['y'=4,'pair'=8,'side'=2,'core'=2,'run'=4] {'core'}, dimensions={0}, use_global_device_ids=true | all-gather | bytes 393216 | tf_op jit(solution)/shard_map/all_gather | solution.py:190
  39.1 0.1 copy.15
  39.2 0.4 shard_map.47
  39.6 15.2 %all_to_all.26 = f32[32,17,1,128]{3,2,1,0:T(1,128)S(1)} all-to-all(f32[32,17,1,128]{3,2,1,0:T(1,128)S(1)} %bitcast.19), channel_id=1, replica_groups=mesh['y'=4,'pair'=8,'side'=2,'core'=2,'run'=4] {'y','run','side'}, dimensions={0} | all-to-all | bytes 557056 | tf_op jit(solution)/shard_map/all_to_all | solution.py:186
  54.8 0.2 reduce_sum.18
  55.0 15.0 %all_to_all.27 = f32[8,17,1,128]{3,2,1,0:T(1,128)S(1)} all-to-all(f32[8,17,1,128]{3,2,1,0:T(1,128)S(1)} %broadcast_in_dim.4), channel_id=1, replica_groups=mesh['y'=4,'pair'=8,'side'=2,'core'=2,'run'=4] {'pair'}, dimensions={0} | all-to-all | bytes 139264 | tf_op jit(solution)/shard_map/all_to_all | solution.py:186
  70.0 0.1 reduce_sum.19
  70.0 0.1 broadcast_in_dim.5
  70.2 11.4 %all_to_all.28 = f32[32,17,1,128]{3,2,1,0:T(1,128)S(1)} all-to-all(f32[32,17,1,128]{3,2,1,0:T(1,128)S(1)} %broadcast_in_dim.5), channel_id=1, replica_groups=mesh['y'=4,'pair'=8,'side'=2,'core'=2,'run'=4] {'y','run','side'}, dimensions={0} | all-to-all | bytes 557056 | tf_op jit(solution)/shard_map/all_to_all | solution.py:186
  81.6 0.0 copy-start
  81.6 6.8 %all_gather.7 = f32[2,544,128]{2,1,0:T(8,128)S(1)} all-gather(f32[1,544,128]{2,1,0:T(8,128)S(1)} %bitcast.24), channel_id=1, replica_groups=mesh['y'=4,'pair'=8,'side'=2,'core'=2,'run'=4] {'core'}, dimensions={0}, use_global_device_ids=true | all-gather | bytes 835584 | tf_op jit(solution)/shard_map/all_gather | solution.py:190
  88.4 0.0 copy-done
  88.4 7.3 %shard_map.48 = f32[64,128]{1,0:T(8,128)S(1)} custom-call(f32[1088,128]{1,0:T(8,128)S(1)} %bitcast.18, f32[64,512]{1,0:T(8,128)S(1)} %bitcast.21, bf16[2,512,128]{2,1,0:T(8,128)(2,1)S(1)} %bitcast.17), custom_call_target="tpu_custom_call" | custom-call | tf_op jit(solution)/shard_map/pallas_call | solution.py:222
  95.8 17.1 %all_to_all.29 = f32[64,1,128]{2,1,0:T(1,128)S(1)} all-to-all(f32[64,1,128]{2,1,0:T(1,128)S(1)} %bitcast.22), channel_id=1, replica_groups=mesh['y'=4,'pair'=8,'side'=2,'core'=2,'run'=4] {'y','pair','side'}, dimensions={0} | all-to-all | bytes 65536 | tf_op jit(solution)/shard_map/all_to_all | solution.py:186
  112.9 0.9 shard_map.49
  (1 shorter events, 0.0 us)
Async XLA Ops:
  81.6 6.8 %copy-start = (f32[512,64]{0,1:T(8,128)S(1)}, f32[512,64]{0,1:T(8,128)}, u32[]{:S(2)}) copy-start(f32[512,64]{0,1:T(8,128)} %param.7) | copy-start | bytes 393220

commit v11 on v10

--- a/solution.py
+++ b/solution.py
@@ -71,8 +71,9 @@
     low_half = lane % K < K // 2
     for chip in range(out_ref.shape[0] // 2):
         first, second = weigh(2 * chip), weigh(2 * chip + 1)
-        low = jnp.where(low_half, first, pltpu.roll(second, K // 2, 1))
-        high = jnp.where(low_half, pltpu.roll(first, LANES - K // 2, 1), second)
+        turned = pltpu.roll(jnp.where(low_half, second, first), K // 2, 1)
+        low = jnp.where(low_half, first, turned)
+        high = jnp.where(low_half, turned, second)
         out_ref[2 * chip] = low.astype(jnp.bfloat16)
         out_ref[2 * chip + 1] = high.astype(jnp.bfloat16)
 
@@ -173,9 +174,11 @@
     chip = lax.broadcasted_iota(jnp.int32, (chips, 4 * chips), 0)
     station = lax.broadcasted_iota(jnp.int32, (chips, 4 * chips), 1)
     parts = parts_ref[...].astype(jnp.bfloat16)
+    core = lax.axis_index("core")
     out = None
     for at in range(4):
-        place = (station == 4 * chip + at).astype(jnp.bfloat16)
+        which = jnp.where(core == 0, at, 1 - at) if at < 2 else at
+        place = (station == 4 * chip + which).astype(jnp.bfloat16)
         lane = K * (at % 2) + K // 2 * (at // 2)
         term = tn(parts[:, lane : lane + K // 2], place)
         out = term if out is None else out + term

time: 114 us -> 114 us (level)
  no operation moved by 1% of the time
where the time goes in v11:
time: 114 us
  blocking collectives  104 us (91%)
  Pallas kernels  9.66 us (8%)
    all_to_all x5, blocking collectives, swap(): return lax.all_to_all(array, axes, 0, 0, tiled=True)  91.7 us
    all_gather x2, blocking collectives, from_both_cores(): return lax.all_gather(array, 'core', axis=0)  11.8 us
    pallas_call x1, Pallas kernels, per_device(): call(factor_kernel, (rank, LANES), jnp.float32, [VMEM] * 3, [pltpu.VMEM((...  7.33 us

profile of v11, /device:TPU:1, one launch (start us, length us, event | category | flops | bytes accessed | tf_op | source)
XLA Modules:
  0.0 113.7 jit_solution(7424163498761567401)
XLA Ops:
  0.0 1.1 shard_map.46
  1.1 33.0 %all_to_all.25 = bf16[64,2,4,128]{3,2,1,0:T(4,128)(2,1)S(1)} all-to-all(bf16[64,2,4,128]{3,2,1,0:T(4,128)(2,1)S(1)} %bitcast.20), channel_id=1, replica_groups=mesh['y'=4,'pair'=8,'side'=2,'core'=2,'run'=4] {'y','pair','side'}, dimensions={0} | all-to-all | bytes 262144 | tf_op jit(solution)/shard_map/all_to_all | solution.py:189
  34.2 5.0 %all_gather.6 = bf16[2,512,128]{2,1,0:T(8,128)(2,1)S(1)} all-gather(bf16[1,512,128]{2,1,0:T(8,128)(2,1)S(1)} %bitcast.26), channel_id=1, replica_groups=mesh['y'=4,'pair'=8,'side'=2,'core'=2,'run'=4] {'core'}, dimensions={0}, use_global_device_ids=true | all-gather | bytes 393216 | tf_op jit(solution)/shard_map/all_gather | solution.py:193
  39.1 0.1 copy.15
  39.2 0.4 shard_map.47
  39.6 15.2 %all_to_all.26 = f32[32,17,1,128]{3,2,1,0:T(1,128)S(1)} all-to-all(f32[32,17,1,128]{3,2,1,0:T(1,128)S(1)} %bitcast.19), channel_id=1, replica_groups=mesh['y'=4,'pair'=8,'side'=2,'core'=2,'run'=4] {'y','run','side'}, dimensions={0} | all-to-all | bytes 557056 | tf_op jit(solution)/shard_map/all_to_all | solution.py:189
  54.8 0.2 reduce_sum.18
  55.0 15.0 %all_to_all.27 = f32[8,17,1,128]{3,2,1,0:T(1,128)S(1)} all-to-all(f32[8,17,1,128]{3,2,1,0:T(1,128)S(1)} %broadcast_in_dim.4), channel_id=1, replica_groups=mesh['y'=4,'pair'=8,'side'=2,'core'=2,'run'=4] {'pair'}, dimensions={0} | all-to-all | bytes 139264 | tf_op jit(solution)/shard_map/all_to_all | solution.py:189
  70.0 0.1 reduce_sum.19
  70.0 0.1 broadcast_in_dim.5
  70.2 11.4 %all_to_all.28 = f32[32,17,1,128]{3,2,1,0:T(1,128)S(1)} all-to-all(f32[32,17,1,128]{3,2,1,0:T(1,128)S(1)} %broadcast_in_dim.5), channel_id=1, replica_groups=mesh['y'=4,'pair'=8,'side'=2,'core'=2,'run'=4] {'y','run','side'}, dimensions={0} | all-to-all | bytes 557056 | tf_op jit(solution)/shard_map/all_to_all | solution.py:189
  81.6 0.0 copy-start
  81.6 6.8 %all_gather.7 = f32[2,544,128]{2,1,0:T(8,128)S(1)} all-gather(f32[1,544,128]{2,1,0:T(8,128)S(1)} %bitcast.24), channel_id=1, replica_groups=mesh['y'=4,'pair'=8,'side'=2,'core'=2,'run'=4] {'core'}, dimensions={0}, use_global_device_ids=true | all-gather | bytes 835584 | tf_op jit(solution)/shard_map/all_gather | solution.py:193
  88.4 0.0 copy-done
  88.5 7.3 %shard_map.48 = f32[64,128]{1,0:T(8,128)S(1)} custom-call(f32[1088,128]{1,0:T(8,128)S(1)} %bitcast.18, f32[64,512]{1,0:T(8,128)S(1)} %bitcast.21, bf16[2,512,128]{2,1,0:T(8,128)(2,1)S(1)} %bitcast.17), custom_call_target="tpu_custom_call" | custom-call | tf_op jit(solution)/shard_map/pallas_call | solution.py:225
  95.8 17.1 %all_to_all.29 = f32[64,1,128]{2,1,0:T(1,128)S(1)} all-to-all(f32[64,1,128]{2,1,0:T(1,128)S(1)} %bitcast.22), channel_id=1, replica_groups=mesh['y'=4,'pair'=8,'side'=2,'core'=2,'run'=4] {'y','pair','side'}, dimensions={0} | all-to-all | bytes 65536 | tf_op jit(solution)/shard_map/all_to_all | solution.py:189
  112.9 0.9 shard_map.49
  (1 shorter events, 0.0 us)
Async XLA Ops:
  81.6 6.8 %copy-start = (f32[512,64]{0,1:T(8,128)S(1)}, f32[512,64]{0,1:T(8,128)}, u32[]{:S(2)}) copy-start(f32[512,64]{0,1:T(8,128)} %param.7) | copy-start | bytes 393220

commit v12 on v10

--- a/solution.py
+++ b/solution.py
@@ -140,6 +140,15 @@
     return jnp.concatenate(rows, axis=0)
 
 
+def with_itself(a):
+    high = a.astype(jnp.bfloat16)
+    rest = a - high.astype(jnp.float32)
+    middle = rest.astype(jnp.bfloat16)
+    low = (rest - middle.astype(jnp.float32)).astype(jnp.bfloat16)
+    mirrored = nt(low, high) + nt(middle, high)
+    return (mirrored + mirrored.T) + nt(middle, middle) + nt(high, high)
+
+
 def factor_kernel(packed_ref, start_ref, fibres_ref, out_ref, gram_ref):
     def put(i, j, block):
         gram_ref[i * 128 : (i + 1) * 128, j * 128 : (j + 1) * 128] = block
@@ -158,7 +167,7 @@
             put(j, i, block.T)
     product = nn(start_ref[...], gram_ref[...], HIGHEST)
     for iteration in range(ITERS):
-        small = nt(product, product, HIGHEST)
+        small = with_itself(product)
         if iteration < ITERS - 1:
             product = nn(product, gram_ref[...], HIGHEST)
         product = nn(inverse_cholesky(small), product, HIGHEST)

time: 114 us -> 114 us (level)
  no operation moved by 1% of the time
where the time goes in v12:
time: 114 us
  blocking collectives  104 us (91%)
  Pallas kernels  9.68 us (8%)
    all_to_all x5, blocking collectives, swap(): return lax.all_to_all(array, axes, 0, 0, tiled=True)  91.7 us
    all_gather x2, blocking collectives, from_both_cores(): return lax.all_gather(array, 'core', axis=0)  11.8 us
    pallas_call x1, Pallas kernels, per_device(): call(factor_kernel, (rank, LANES), jnp.float32, [VMEM] * 3, [pltpu.VMEM((...  7.33 us

profile of v12, /device:TPU:1, one launch (start us, length us, event | category | flops | bytes accessed | tf_op | source)
XLA Modules:
  0.0 113.7 jit_solution(4361366227932158478)
XLA Ops:
  0.0 1.1 shard_map.46
  1.1 33.0 %all_to_all.25 = bf16[64,2,4,128]{3,2,1,0:T(4,128)(2,1)S(1)} all-to-all(bf16[64,2,4,128]{3,2,1,0:T(4,128)(2,1)S(1)} %bitcast.20), channel_id=1, replica_groups=mesh['y'=4,'pair'=8,'side'=2,'core'=2,'run'=4] {'y','pair','side'}, dimensions={0} | all-to-all | bytes 262144 | tf_op jit(solution)/shard_map/all_to_all | solution.py:195
  34.2 5.0 %all_gather.6 = bf16[2,512,128]{2,1,0:T(8,128)(2,1)S(1)} all-gather(bf16[1,512,128]{2,1,0:T(8,128)(2,1)S(1)} %bitcast.26), channel_id=1, replica_groups=mesh['y'=4,'pair'=8,'side'=2,'core'=2,'run'=4] {'core'}, dimensions={0}, use_global_device_ids=true | all-gather | bytes 393216 | tf_op jit(solution)/shard_map/all_gather | solution.py:199
  39.1 0.1 copy.15
  39.2 0.4 shard_map.47
  39.6 15.2 %all_to_all.26 = f32[32,17,1,128]{3,2,1,0:T(1,128)S(1)} all-to-all(f32[32,17,1,128]{3,2,1,0:T(1,128)S(1)} %bitcast.19), channel_id=1, replica_groups=mesh['y'=4,'pair'=8,'side'=2,'core'=2,'run'=4] {'y','run','side'}, dimensions={0} | all-to-all | bytes 557056 | tf_op jit(solution)/shard_map/all_to_all | solution.py:195
  54.8 0.2 reduce_sum.18
  55.0 15.0 %all_to_all.27 = f32[8,17,1,128]{3,2,1,0:T(1,128)S(1)} all-to-all(f32[8,17,1,128]{3,2,1,0:T(1,128)S(1)} %broadcast_in_dim.4), channel_id=1, replica_groups=mesh['y'=4,'pair'=8,'side'=2,'core'=2,'run'=4] {'pair'}, dimensions={0} | all-to-all | bytes 139264 | tf_op jit(solution)/shard_map/all_to_all | solution.py:195
  70.0 0.1 reduce_sum.19
  70.0 0.1 broadcast_in_dim.5
  70.2 11.4 %all_to_all.28 = f32[32,17,1,128]{3,2,1,0:T(1,128)S(1)} all-to-all(f32[32,17,1,128]{3,2,1,0:T(1,128)S(1)} %broadcast_in_dim.5), channel_id=1, replica_groups=mesh['y'=4,'pair'=8,'side'=2,'core'=2,'run'=4] {'y','run','side'}, dimensions={0} | all-to-all | bytes 557056 | tf_op jit(solution)/shard_map/all_to_all | solution.py:195
  81.6 0.0 copy-start
  81.6 6.8 %all_gather.7 = f32[2,544,128]{2,1,0:T(8,128)S(1)} all-gather(f32[1,544,128]{2,1,0:T(8,128)S(1)} %bitcast.24), channel_id=1, replica_groups=mesh['y'=4,'pair'=8,'side'=2,'core'=2,'run'=4] {'core'}, dimensions={0}, use_global_device_ids=true | all-gather | bytes 835584 | tf_op jit(solution)/shard_map/all_gather | solution.py:199
  88.4 0.0 copy-done
  88.4 7.3 %shard_map.48 = f32[64,128]{1,0:T(8,128)S(1)} custom-call(f32[1088,128]{1,0:T(8,128)S(1)} %bitcast.18, f32[64,512]{1,0:T(8,128)S(1)} %bitcast.21, bf16[2,512,128]{2,1,0:T(8,128)(2,1)S(1)} %bitcast.17), custom_call_target="tpu_custom_call" | custom-call | tf_op jit(solution)/shard_map/pallas_call | solution.py:231
  95.8 17.1 %all_to_all.29 = f32[64,1,128]{2,1,0:T(1,128)S(1)} all-to-all(f32[64,1,128]{2,1,0:T(1,128)S(1)} %bitcast.22), channel_id=1, replica_groups=mesh['y'=4,'pair'=8,'side'=2,'core'=2,'run'=4] {'y','pair','side'}, dimensions={0} | all-to-all | bytes 65536 | tf_op jit(solution)/shard_map/all_to_all | solution.py:195
  112.9 0.9 shard_map.49
  (1 shorter events, 0.0 us)
Async XLA Ops:
  81.6 6.8 %copy-start = (f32[512,64]{0,1:T(8,128)S(1)}, f32[512,64]{0,1:T(8,128)}, u32[]{:S(2)}) copy-start(f32[512,64]{0,1:T(8,128)} %param.7) | copy-start | bytes 393220
